TPU v7x, 32 devices: a whole 2x2x4 slice. The times are simulated.
32 devices in a mesh: tm: 8 (over z, x), rows: 4 (over y, core).
Axes of the slice: x: 2, y: 2, z: 4, core: 2. Of those that a mesh axis runs over, the one named last changes fastest.
Arguments:
- tile_values: bfloat16 [16384, 128, 128], P(('tm', 'rows')), may hold values from -6 to 6
- tile_users: int32 [16384], P(('tm', 'rows')), may hold values from 0 to 31
- tile_items: int32 [16384], P(('tm', 'rows')), may hold values from 0 to 31
- tile_steps: int32 [16384], P(('tm', 'rows')), may hold values from 0 to 7
- tile_count: int32 [32], P(('tm', 'rows')), may hold values from 64 to 512, as said below
- users_ask: int32 [1024, 1], P(('tm', 'rows')), may hold values from 0 to 7, as said below
- items_ask: int32 [1024, 1], P(('tm', 'rows')), may hold values from 0 to 7, as said below
- user_factor: float32 [256, 64, 128], P(('tm', 'rows')), may hold values from -6 to 6
- item_factor: float32 [256, 64, 128], P(('tm', 'rows')), may hold values from -6 to 6
- time_factor: float32 [64, 64], P('tm'), may hold values from -2 to 2
- core: float32 [64, 64, 64], replicated, may hold values from -0.25 to 0.25
Outputs:
- grad_users: float32 [256, 64, 128], P(('tm', 'rows'))
- grad_items: float32 [256, 64, 128], P(('tm', 'rows'))
- grad_time: float32 [64, 64], P('tm')
- grad_core: float32 [64, 64, 64], replicated
Inputs may be any that keep to these rules, and one draw needn't show every extreme that they name: `users_ask`: each row holds 1 distinct local block numbers of the owner that the row names. `items_ask`: each row holds 1 distinct local block numbers of the owner that the row names. `tile_count`: slots of a device at or past its count are padding; some device is full.
All inputs are finite; a program needn't handle non-finite values.
Results may differ from a plain program's by a relative error of at most 0.0003.
Values sent between devices are 32-bit elements; how exact they have to be, the bound alone decides.
A program may use at most 128 MiB of HBM per device.

v0:
```python
import jax
import jax.numpy as jnp
from jax import lax
from jax.sharding import PartitionSpec as P

HIGH = lax.Precision.HIGHEST
user_scale = 0.125
time_scale = 1.0 / 2048.0
core_scale = 1.0 / 4096.0


def shards(
    tile_values,
    tile_users,
    tile_items,
    tile_steps,
    tile_count,
    users_ask,
    items_ask,
    user_factor,
    item_factor,
    time_factor,
    core,
):
    count_tm = lax.axis_size("tm")
    count_rows = lax.axis_size("rows")
    owners = count_tm * count_rows
    slot_cap = users_ask.shape[1]
    rank = user_factor.shape[1]
    width = user_factor.shape[2]
    blocks_own = user_factor.shape[0]
    step_count = time_factor.shape[0]
    tile_slots = tile_values.shape[0]
    ask_user = lax.all_to_all(users_ask, ("tm", "rows"), split_axis=0, concat_axis=0, tiled=True)
    ask_item = lax.all_to_all(items_ask, ("tm", "rows"), split_axis=0, concat_axis=0, tiled=True)
    found_user = jnp.take(user_factor, ask_user, axis=0)
    found_item = jnp.take(item_factor, ask_item, axis=0)
    back_user = lax.all_to_all(found_user, ("tm", "rows"), split_axis=0, concat_axis=0, tiled=True)
    back_item = lax.all_to_all(found_item, ("tm", "rows"), split_axis=0, concat_axis=0, tiled=True)
    fetched_user = back_user
    fetched_item = back_item
    held_user = ask_user
    held_item = ask_item
    fetched_user = fetched_user.reshape(owners * slot_cap, rank, width)
    fetched_item = fetched_item.reshape(owners * slot_cap, rank, width)
    held_user = held_user.reshape(owners * slot_cap)
    held_item = held_item.reshape(owners * slot_cap)
    step_cores = jnp.einsum("pqr,sr->spq", core, time_factor, precision=HIGH)
    block_size = min(64, tile_slots)
    live_count = tile_count[0]
    block_total = (live_count + block_size - 1) // block_size
    step_ids = jnp.arange(step_count, dtype=jnp.int32)

    def one_block(index, carry):
        grad_left, grad_right, step_sums = carry
        start = index * block_size
        values = lax.dynamic_slice_in_dim(tile_values, start, block_size, 0).astype(jnp.float32)
        slots_user = lax.dynamic_slice_in_dim(tile_users, start, block_size, 0)
        slots_item = lax.dynamic_slice_in_dim(tile_items, start, block_size, 0)
        local_steps = lax.dynamic_slice_in_dim(tile_steps, start, block_size, 0)
        picker = (local_steps[:, None] == step_ids[None, :]).astype(jnp.float32)
        cores = jnp.einsum("ts,spq->tpq", picker, step_cores, precision=HIGH)
        left = jnp.take(fetched_user, slots_user, axis=0)
        right = jnp.take(fetched_item, slots_item, axis=0)
        live = (start + jnp.arange(block_size, dtype=jnp.int32) < live_count).astype(jnp.float32)
        mixed = jnp.einsum("tpq,tqj->tpj", cores, right, precision=HIGH)
        guess = jnp.einsum("tpi,tpj->tij", left, mixed, precision=HIGH)
        resid = (guess - values) * live[:, None, None]
        grad_u = jnp.einsum("tij,tpj->tpi", resid, mixed, precision=HIGH)
        across = jnp.einsum("tpi,tpq->tqi", left, cores, precision=HIGH)
        grad_v = jnp.einsum("tij,tqi->tqj", resid, across, precision=HIGH)
        inner = jnp.einsum("tpi,tij->tpj", left, resid, precision=HIGH)
        dcore = jnp.einsum("tpj,tqj->tpq", inner, right, precision=HIGH)
        grad_left = grad_left.at[slots_user].add(grad_u)
        grad_right = grad_right.at[slots_item].add(grad_v)
        step_sums = step_sums + jnp.einsum("ts,tpq->spq", picker, dcore, precision=HIGH)
        return (grad_left, grad_right, step_sums)

    start_carry = (
        jnp.zeros((owners * slot_cap, rank, width), jnp.float32),
        jnp.zeros((owners * slot_cap, rank, width), jnp.float32),
        jnp.zeros((step_count, rank, rank), jnp.float32),
    )
    slot_left, slot_right, step_sums = lax.fori_loop(0, block_total, one_block, start_carry)
    back_left, back_right = (
        lax.all_to_all(
            slot_left.reshape(owners, slot_cap, rank, width),
            ("tm", "rows"),
            split_axis=0,
            concat_axis=0,
            tiled=True,
        ),
        lax.all_to_all(
            slot_right.reshape(owners, slot_cap, rank, width),
            ("tm", "rows"),
            split_axis=0,
            concat_axis=0,
            tiled=True,
        ),
    )
    own_ids = jnp.arange(blocks_own, dtype=jnp.int32)
    owner_user = (held_user[:, None] == own_ids[None, :]).astype(jnp.float32)
    owner_item = (held_item[:, None] == own_ids[None, :]).astype(jnp.float32)
    grad_users = user_scale * jnp.einsum(
        "nb,npi->bpi", owner_user, back_left.reshape(owners * slot_cap, rank, width), precision=HIGH
    )
    grad_items = user_scale * jnp.einsum(
        "nb,npi->bpi",
        owner_item,
        back_right.reshape(owners * slot_cap, rank, width),
        precision=HIGH,
    )
    slice_total = lax.psum(step_sums, "rows")
    grad_time = time_scale * jnp.einsum("spq,pqr->sr", slice_total, core, precision=HIGH)
    own_term = jnp.einsum("spq,sr->pqr", step_sums, time_factor, precision=HIGH)
    core_total = lax.psum(own_term, ("tm", "rows"))
    grad_core = core_scale * core_total
    return (grad_users, grad_items, grad_time, grad_core)


def solution(mesh):
    in_specs = (
        P(("tm", "rows"), None, None),
        P(("tm", "rows")),
        P(("tm", "rows")),
        P(("tm", "rows")),
        P(("tm", "rows")),
        P(("tm", "rows"), None),
        P(("tm", "rows"), None),
        P(("tm", "rows"), None, None),
        P(("tm", "rows"), None, None),
        P("tm", None),
        P(),
    )
    out_specs = (P(("tm", "rows"), None, None), P(("tm", "rows"), None, None), P("tm", None), P())
    return jax.shard_map(shards, mesh=mesh, in_specs=in_specs, out_specs=out_specs, check_vma=False)
```

profile of v0, /device:TPU:0, one launch (start us, length us, event | category | flops | bytes accessed | tf_op | source)
XLA Modules:
  0.0 943.3 jit_solution(2595082677469671045)
XLA Ops:
  7.2 1.5 copy.31
  8.7 7.3 all-to-all-start.1
  16.0 1.3 copy.30
  17.3 5.7 all-to-all-done.1
  23.0 2.5 all-to-all-start
  25.6 0.7 reduce.1
  26.3 1.6 gather_fusion.2
  27.9 1.1 bitcast_select_fusion.1
  29.0 3.7 all-to-all-done
  32.7 2.6 all-to-all-start.2
  35.3 0.7 reduce
  36.0 1.6 gather_fusion.3
  37.6 2.3 bitcast_select_fusion
  39.9 21.6 %all-to-all-done.2 = f32[32,1,64,128]{3,2,1,0:T(8,128)S(1)} async-done(((f32[32,1,64,128]{3,2,1,0:T(8,128)}), f32[32,1,64,128]{3,2,1,0:T(8,128)S(1)}, u32[]{:S(2)}, u32[]{:S(2)}) %all-to-all-start.2) | async-done | bytes 1048608 | tf_op jit(solution)/shard_map/all_to_all | solution.py:39
  61.5 3.7 all-to-all-start.3
  65.9 5.7 fusion.44
  71.6 19.8 %all-to-all-done.3 = f32[32,1,64,128]{3,2,1,0:T(8,128)} async-done(((f32[32,1,64,128]{3,2,1,0:T(8,128)}), f32[32,1,64,128]{3,2,1,0:T(8,128)}, u32[]{:S(2)}, u32[]{:S(2)}) %all-to-all-start.3) | async-done | bytes 1048608 | tf_op jit(solution)/shard_map/all_to_all | solution.py:38
  91.6 1.2 broadcast.49
  92.8 103.1 %while.15 = (s32[]{:T(128)}, f32[32,64,128]{2,1,0:T(8,128)}, f32[32,64,128]{2,1,0:T(8,128)S(1)}, f32[8,64,64]{2,0,1:T(8,128)S(1)}, s32[]{:T(128)}, /*index=5*/s3...) while((s32[]{:T(128)}, f32[32,64,128]{2,1,0:T(8,128)}, ...), condition=%wide.region_3.6_spmd.clone, body=%wide.region_0.5_spmd.clone.sunk | while | flops 4486369280 | bytes 97923816 | solution.py:84
  116.6 0.8 dynamic_slice.24
  117.4 0.8 compare_and_fusion.3
  118.2 3.2 gather_fusion.1
  121.4 3.2 gather_fusion
  124.7 3.3 fusion.114
  128.0 3.3 copy.51
  131.3 5.9 fusion.115
  137.3 2.3 fusion.117
  139.6 8.9 subtract_multiply_fusion.2
  148.5 3.9 fusion.119
  152.4 3.4 fusion.120
  155.9 2.0 fusion.121
  157.9 5.2 fusion.118
  163.1 9.5 %fusion.116 = f32[64,64,128]{2,1,0:T(8,128)} fusion(f32[64,64,128]{2,1,0:T(8,128)S(1)} %fusion.115, f32[64,128,128]{2,1,0:T(8,128)S(1)} %subtract_multiply_fusion.2), kind=kOutput, calls=%fused_computation.76.clone.1 | convolution fusion | flops 805306368 | bytes 8388608 | tf_op jit(solution)/shard_map/while/body/tij,tpj->tpi/dot_general | solution.py:69
  172.6 10.3 %scatter_fusion = f32[32,64,128]{2,1,0:T(8,128)} fusion(f32[32,64,128]{2,1,0:T(8,128)} %get-tuple-element.263, s32[64]{0:T(128)S(1)} %get-tuple-element.241, f32[64,64,128]{2,1,0:T(8,128)} %fusion.116), kind=kCustom, calls=%fused_computation.4.clone.clone.1 | custom fusion | flops 524288 | bytes 6291712 | tf_op jit(solution)/shard_map/while/body/scatter-add | solution.py:74
  183.0 7.0 scatter_fusion.1
  195.9 546.8 %all_to_all.44 = f32[32,1,64,128]{3,2,1,0:T(8,128)} all-to-all(f32[32,1,64,128]{3,2,1,0:T(8,128)S(1)} %bitcast.95), channel_id=1, replica_groups=mesh['tm'=8,'rows'=4] {'tm','rows'}, dimensions={0} | all-to-all | bytes 2097152 | tf_op jit(solution)/shard_map/all_to_all | solution.py:93
  742.7 3.6 all-to-all-start.4
  746.3 4.8 fusion.42
  751.1 0.7 all-reduce.3.cloned.1.call-update
  751.8 0.7 all-reduce.5.cloned.1.call-update
  752.5 36.2 %all-reduce.3.cloned.1.call-done = f32[8,64,64]{2,0,1:T(8,128)} async-done(((f32[8,64,64]{2,0,1:T(8,128)}), f32[8,64,64]{2,0,1:T(8,128)}) %all-reduce.3.cloned.1.call-update) | async-done | bytes 131088 | tf_op jit(solution)/shard_map/psum | solution.py:113
  788.7 2.7 fusion.37
  791.4 137.9 %all-reduce.5.cloned.1.call-done = f32[64,64,64]{2,1,0:T(8,128)} async-done(((f32[64,64,64]{2,1,0:T(8,128)}), f32[64,64,64]{2,1,0:T(8,128)}) %all-reduce.5.cloned.1.call-update) | async-done | bytes 1048592 | tf_op jit(solution)/shard_map/psum | solution.py:116
  929.3 3.3 broadcast_multiply_fusion
  932.6 1.0 convolution_multiply_fusion
  933.7 0.8 copy.35
  934.4 1.0 convolution_multiply_fusion.1
  935.5 0.8 copy.34
  (32 shorter events, 0.9 us)
Async XLA Ops:
  7.2 58.7 %copy-start = (f32[64,64,64]{2,1,0:T(8,128)S(1)}, f32[64,64,64]{2,1,0:T(8,128)}, u32[]{:S(2)}) copy-start(f32[64,64,64]{2,1,0:T(8,128)} %param.27) | copy-start | bytes 3145732
  8.7 14.4 %all-to-all-start.1 = ((s32[32,1,1]{2,1,0:T(1,128)}), s32[32,1,1]{2,1,0:T(1,128)S(1)}, u32[]{:S(2)}, u32[]{:S(2)}) async-start(s32[32,1,1]{2,1,0:T(1,128)} %copy.31), calls=%async_computation.1 | async-start | bytes 32768 | tf_op jit(solution)/shard_map/all_to_all | solution.py:35
  23.0 9.6 %all-to-all-start = ((s32[32,1,1]{2,1,0:T(1,128)}), s32[32,1,1]{2,1,0:T(1,128)S(1)}, u32[]{:S(2)}, u32[]{:S(2)}) async-start(s32[32,1,1]{2,1,0:T(1,128)} %copy.30), calls=%async_computation | async-start | bytes 32768 | tf_op jit(solution)/shard_map/all_to_all | solution.py:34
  27.9 8.1 copy-start.6
  32.7 28.9 %all-to-all-start.2 = ((f32[32,1,64,128]{3,2,1,0:T(8,128)}), f32[32,1,64,128]{3,2,1,0:T(8,128)S(1)}, u32[]{:S(2)}, u32[]{:S(2)}) async-start(f32[32,1,64,128]{3,2,1,0:T(8,128)} %bitcast_select_fusion.1), calls=%async_computation.2 | async-start | bytes 2097152 | tf_op jit(solution)/shard_map/all_to_all | solution.py:39
  37.6 28.3 %copy-start.8 = (f32[8,64]{1,0:T(8,128)S(1)}, f32[8,64]{1,0:T(8,128)}, u32[]{:S(2)}) copy-start(f32[8,64]{1,0:T(8,128)} %param.26) | copy-start | bytes 6148
  61.5 10.0 %copy-start.4 = (f32[32,1,64,128]{3,2,1,0:T(8,128)}, f32[32,1,64,128]{3,2,1,0:T(8,128)S(1)}, u32[]{:S(2)}) copy-start(f32[32,1,64,128]{3,2,1,0:T(8,128)S(1)} %all-to-all-done.2) | copy-start | bytes 3145732
  61.5 29.9 %all-to-all-start.3 = ((f32[32,1,64,128]{3,2,1,0:T(8,128)}), f32[32,1,64,128]{3,2,1,0:T(8,128)}, u32[]{:S(2)}, u32[]{:S(2)}) async-start(f32[32,1,64,128]{3,2,1,0:T(8,128)} %bitcast_select_fusion), calls=%async_computation.3 | async-start | bytes 2097152 | tf_op jit(solution)/shard_map/all_to_all | solution.py:38
  131.3 5.9 copy-start.1
  131.3 5.9 copy-start.3
  148.5 3.9 copy-start.2
  195.9 550.4 %copy-start.5 = (f32[8,64,64]{2,0,1:T(8,128)}, f32[8,64,64]{2,0,1:T(8,128)S(1)}, u32[]{:S(2)}) copy-start(f32[8,64,64]{2,0,1:T(8,128)S(1)} %get-tuple-element.83) | copy-start | bytes 393220
  742.7 191.8 %all-to-all-start.4 = ((f32[32,1,64,128]{3,2,1,0:T(8,128)}), f32[32,1,64,128]{3,2,1,0:T(8,128)S(1)}, u32[]{:S(2)}, u32[]{:S(2)}) async-start(f32[32,1,64,128]{3,2,1,0:T(8,128)} %bitcast.96), calls=%async_computation.4 | async-start | bytes 2097152 | tf_op jit(solution)/shard_map/all_to_all | solution.py:86
  751.1 37.7 %all-reduce.3.cloned.1.call-start = ((), (), s32[]{:S(2)}) async-start(), calls=%async_computation.6 | async-start | bytes 524288 | tf_op jit(solution)/shard_map/psum | solution.py:113
  751.8 177.5 %all-reduce.5.cloned.1.call-start = ((), (), s32[]{:S(2)}) async-start(), calls=%async_computation.7 | async-start | bytes 4194304 | tf_op jit(solution)/shard_map/psum | solution.py:116
  929.3 3.3 copy-start.7
Sparse Core Ops, SparseCore 0:
  754.8 33.8 all-reduce.2
  795.5 133.7 all-reduce.4
where the time goes:
time: 952 us; the launch traced here: 943 us
  blocking collectives  547 us (57%)
  waiting for transfers between devices  226 us (24%)
  matrix products  59.7 us (6%)
  loops' own time  29.2 us (3%)
  other arithmetic  26.9 us (3%)
  starting transfers between devices  19.8 us (2%)
  local copies, waits for them, and re-layouts  19.4 us (2%)
  between operations  15.1 us (2%)
    all_to_all x1, blocking collectives, shards(): lax.all_to_all(slot_right.reshape(owners, slot_cap, rank, width), ('tm',...  547 us
    psum x1, waiting for transfers between devices, shards(): core_total = lax.psum(own_term, ('tm', 'rows'))  138 us
    psum x1, waiting for transfers between devices, shards(): slice_total = lax.psum(step_sums, 'rows')  36.2 us
    another operation x1, loops' own time, shards(): lax.fori_loop(0, block_total, one_block, start_carry)  29.2 us
    all_to_all x1, waiting for transfers between devices, shards(): lax.all_to_all(found_item, ('tm', 'rows'), split_axis=0, concat_axis=0, t...  21.6 us
    all_to_all x1, waiting for transfers between devices, shards(): lax.all_to_all(found_user, ('tm', 'rows'), split_axis=0, concat_axis=0, t...  19.8 us
  transfers between devices with their start and end apart: 7, of which 6 were waited for; matrix products, arithmetic and copies ran while one was open for 3% of the time, Pallas kernels for 0%

commit v1 on v0

v1 whole, which is shorter than its diff:
```python
import functools

import jax
import jax.numpy as jnp
from jax import lax
from jax.experimental import pallas as pl
from jax.experimental.pallas import tpu as pltpu
from jax.sharding import PartitionSpec as P

HIGH = lax.Precision.HIGHEST
user_scale = 0.125
time_scale = 1.0 / 2048.0
core_scale = 1.0 / 4096.0
BOTH = ("tm", "rows")


def split(x):
    hi = x.astype(jnp.bfloat16)
    lo = (x - hi.astype(jnp.float32)).astype(jnp.bfloat16)
    return hi, lo


def split_outside(x):
    hi = lax.reduce_precision(x, 8, 7)
    return hi.astype(jnp.bfloat16), (x - hi).astype(jnp.bfloat16)


def mm(a, b):
    return jnp.dot(a, b, preferred_element_type=jnp.float32)


def tile_kernel(
    chunk, group, steps, rank,
    users, items, tsteps, count,
    values, left, right, c4, ct2, cq,
    out_u, out_v, out_d,
    u2, ut2, vt2, m2, psum, qsum,
):
    slots = left.shape[0]
    width = left.shape[2]
    step = pl.program_id(0)

    @pl.when(step == 0)
    def prepare():
        @pl.loop(0, slots)
        def one_slot(k):
            hi, lo = split(left[k])
            u2[k] = jnp.concatenate([hi, lo], 0)
            both = jnp.concatenate([hi.astype(jnp.float32), lo.astype(jnp.float32)], 0)
            ut2[k] = both.T.astype(jnp.bfloat16)
            hi, lo = split(right[k])
            both = jnp.concatenate([hi.astype(jnp.float32), lo.astype(jnp.float32)], 0)
            vt2[k] = both.T.astype(jnp.bfloat16)
            mixed = mm(c4[...], jnp.concatenate([hi, hi, lo, lo], 0))
            mhi, mlo = split(mixed)
            for s in range(steps):
                m2[k * steps + s, 0:rank, :] = mhi[s * rank:(s + 1) * rank]
                m2[k * steps + s, rank:2 * rank, :] = mlo[s * rank:(s + 1) * rank]
            psum[k] = jnp.zeros((steps * rank, width), jnp.float32)
            qsum[k] = jnp.zeros((width, steps * 2 * rank), jnp.float32)

    base = step * chunk
    live = jnp.clip(count[0] - base, 0, chunk)

    @pl.loop(0, (live + group - 1) // group)
    def one_group(g):
        first = g * group
        done = []
        for k in range(group):
            t = base + first + k
            u, v, s = users[t], items[t], tsteps[t]
            m = m2[v * steps + s]
            mhi, mlo = m[:rank], m[rank:]
            ut = ut2[u]
            guess = mm(
                jnp.concatenate([ut, ut], 1), jnp.concatenate([mhi, mhi, mlo, mlo], 0)
            )
            resid = guess - values[first + k].astype(jnp.float32)
            resid = jnp.where(first + k < live, resid, 0.0)
            rhi, rlo = split(resid)
            ul = u2[u]
            vt = vt2[v]
            w = mm(jnp.concatenate([ul, ul], 1), jnp.concatenate([rhi, rlo], 0))
            z = mm(jnp.concatenate([rhi, rlo], 1), jnp.concatenate([vt, vt], 0))
            done.append((u, v, s, w[:rank] + w[rank:], z))
        for u, v, s, w, z in done:
            at_p = pl.ds(pl.multiple_of(s * rank, rank), rank)
            psum[v, at_p, :] += w
            at_q = pl.ds(pl.multiple_of(s * 2 * rank, 2 * rank), 2 * rank)
            qsum[u, :, at_q] += z

    @pl.when(step == pl.num_programs(0) - 1)
    def finish():
        out_d[...] = jnp.zeros(out_d.shape, jnp.float32)

        @pl.loop(0, slots)
        def one_slot(k):
            hi, lo = split(psum[k])
            g1 = mm(ct2[...], hi)
            out_v[k] = g1[:rank] + g1[rank:] + mm(ct2[0:rank, :], lo)
            vt = vt2[k]
            out_d[...] += mm(
                jnp.concatenate([hi, lo], 1), jnp.concatenate([vt, vt], 0)
            )
            qhi, qlo = split(qsum[k])
            g2 = (mm(qhi, cq[...]) + mm(qlo, cq[...])).T
            out_u[k] = g2[:rank] + g2[rank:]


def tiles_in_kernel(values, users, items, tsteps, count, left, right, cores):
    slots, rank, width = left.shape
    steps = cores.shape[0]
    total = values.shape[0]
    chunk = 32
    group = 8
    chi, clo = split_outside(cores)
    flat_hi, flat_lo = chi.reshape(steps * rank, rank), clo.reshape(steps * rank, rank)
    c4 = jnp.concatenate([flat_hi, flat_lo, flat_hi, flat_lo], 1)
    ct2 = jnp.concatenate([flat_hi.T, flat_lo.T], 0)
    turned = jnp.concatenate([jnp.swapaxes(chi, 1, 2), jnp.swapaxes(clo, 1, 2)], 2)
    cq = jnp.concatenate([turned, turned], 1).reshape(steps * 2 * rank, 2 * rank)

    def values_at(i, users, items, tsteps, count):
        last = jnp.maximum((count[0] + chunk - 1) // chunk - 1, 0)
        return (jnp.minimum(i, last), 0, 0)

    whole = pl.BlockSpec(memory_space=pltpu.VMEM)
    return pl.pallas_call(
        functools.partial(tile_kernel, chunk, group, steps, rank),
        grid_spec=pltpu.PrefetchScalarGridSpec(
            num_scalar_prefetch=4,
            grid=(total // chunk,),
            in_specs=[pl.BlockSpec((chunk, width, width), values_at)] + [whole] * 5,
            out_specs=[whole] * 3,
            scratch_shapes=[
                pltpu.VMEM((slots, 2 * rank, width), jnp.bfloat16),
                pltpu.VMEM((slots, width, 2 * rank), jnp.bfloat16),
                pltpu.VMEM((slots, width, 2 * rank), jnp.bfloat16),
                pltpu.VMEM((slots * steps, 2 * rank, width), jnp.bfloat16),
                pltpu.VMEM((slots, steps * rank, width), jnp.float32),
                pltpu.VMEM((slots, width, steps * 2 * rank), jnp.float32),
            ],
        ),
        out_shape=[
            jax.ShapeDtypeStruct((slots, rank, width), jnp.float32),
            jax.ShapeDtypeStruct((slots, rank, width), jnp.float32),
            jax.ShapeDtypeStruct((steps * rank, 2 * rank), jnp.float32),
        ],
        compiler_params=pltpu.CompilerParams(
            dimension_semantics=("arbitrary",), vmem_limit_bytes=56 * 2**20
        ),
        name="tiles",
    )(users, items, tsteps, count, values, left, right, c4, ct2, cq)


def tiles_in_loop(values_all, users, items, tsteps, count, left_all, right_all, step_cores):
    slots, rank, width = left_all.shape
    step_count = step_cores.shape[0]
    block_size = min(64, values_all.shape[0])
    live_count = count[0]
    step_ids = jnp.arange(step_count, dtype=jnp.int32)

    def one_block(index, carry):
        grad_left, grad_right, step_sums = carry
        start = index * block_size
        values = lax.dynamic_slice_in_dim(values_all, start, block_size, 0).astype(jnp.float32)
        slots_user = lax.dynamic_slice_in_dim(users, start, block_size, 0)
        slots_item = lax.dynamic_slice_in_dim(items, start, block_size, 0)
        local_steps = lax.dynamic_slice_in_dim(tsteps, start, block_size, 0)
        picker = (local_steps[:, None] == step_ids[None, :]).astype(jnp.float32)
        cores = jnp.take(step_cores, local_steps, axis=0)
        left = jnp.take(left_all, slots_user, axis=0)
        right = jnp.take(right_all, slots_item, axis=0)
        live = (start + jnp.arange(block_size, dtype=jnp.int32) < live_count).astype(jnp.float32)
        mixed = jnp.einsum("tpq,tqj->tpj", cores, right, precision=HIGH)
        guess = jnp.einsum("tpi,tpj->tij", left, mixed, precision=HIGH)
        resid = (guess - values) * live[:, None, None]
        grad_u = jnp.einsum("tij,tpj->tpi", resid, mixed, precision=HIGH)
        across = jnp.einsum("tpi,tpq->tqi", left, cores, precision=HIGH)
        grad_v = jnp.einsum("tij,tqi->tqj", resid, across, precision=HIGH)
        inner = jnp.einsum("tpi,tij->tpj", left, resid, precision=HIGH)
        dcore = jnp.einsum("tpj,tqj->tpq", inner, right, precision=HIGH)
        grad_left = grad_left.at[slots_user].add(grad_u)
        grad_right = grad_right.at[slots_item].add(grad_v)
        step_sums = step_sums + jnp.einsum("ts,tpq->spq", picker, dcore, precision=HIGH)
        return (grad_left, grad_right, step_sums)

    carry = (
        jnp.zeros((slots, rank, width), jnp.float32),
        jnp.zeros((slots, rank, width), jnp.float32),
        jnp.zeros((step_count, rank, rank), jnp.float32),
    )
    return lax.fori_loop(0, (live_count + block_size - 1) // block_size, one_block, carry)


def shards(
    tile_values,
    tile_users,
    tile_items,
    tile_steps,
    tile_count,
    users_ask,
    items_ask,
    user_factor,
    item_factor,
    time_factor,
    core,
):
    count_tm = lax.axis_size("tm")
    count_rows = lax.axis_size("rows")
    owners = count_tm * count_rows
    cap = users_ask.shape[1]
    rank = user_factor.shape[1]
    width = user_factor.shape[2]
    blocks_own = user_factor.shape[0]
    steps = time_factor.shape[0]
    slots = owners * cap

    exchange = functools.partial(
        lax.all_to_all, axis_name=BOTH, split_axis=0, concat_axis=0, tiled=True
    )
    held = exchange(jnp.concatenate([users_ask, items_ask], 1))
    held_user, held_item = held[:, :cap], held[:, cap:]
    found = jnp.concatenate(
        [jnp.take(user_factor, held_user, axis=0), jnp.take(item_factor, held_item, axis=0)], 1
    )
    back = exchange(found)
    left = back[:, :cap].reshape(slots, rank, width)
    right = back[:, cap:].reshape(slots, rank, width)
    cores = jnp.einsum("pqr,sr->spq", core, time_factor, precision=HIGH)
    time_all = lax.all_gather(time_factor, "tm", axis=0, tiled=True)

    if slots <= 32 and tile_values.shape[0] % 32 == 0:
        part_u, part_v, twice = tiles_in_kernel(
            tile_values, tile_users, tile_items, tile_steps, tile_count, left, right, cores
        )
        step_sums = (twice[:, :rank] + twice[:, rank:]).reshape(steps, rank, rank)
    else:
        part_u, part_v, step_sums = tiles_in_loop(
            tile_values, tile_users, tile_items, tile_steps, tile_count, left, right, cores
        )

    own_steps = lax.psum_scatter(
        step_sums.reshape(steps * rank * rank // 128, 128), "rows", scatter_dimension=0, tiled=True
    )
    every = lax.all_gather(own_steps, BOTH, axis=0, tiled=True)
    every = every.reshape(count_tm * steps, rank, rank)
    returned = exchange(
        jnp.concatenate(
            [part_u.reshape(owners, cap, rank, width), part_v.reshape(owners, cap, rank, width)], 1
        )
    )
    own_ids = jnp.arange(blocks_own, dtype=jnp.int32)

    def to_owner(ids, terms):
        pick = (ids.reshape(slots)[:, None] == own_ids[None, :]).astype(jnp.float32)
        return user_scale * jnp.einsum(
            "nb,npi->bpi", pick, terms.reshape(slots, rank, width), precision=HIGH
        )

    grad_users = to_owner(held_user, returned[:, :cap])
    grad_items = to_owner(held_item, returned[:, cap:])
    mine = lax.dynamic_slice_in_dim(every, lax.axis_index("tm") * steps, steps, 0)
    grad_time = time_scale * jnp.einsum("spq,pqr->sr", mine, core, precision=HIGH)
    grad_core = core_scale * jnp.einsum("spq,sr->pqr", every, time_all, precision=HIGH)
    return (grad_users, grad_items, grad_time, grad_core)


def solution(mesh):
    in_specs = (
        P(BOTH, None, None),
        P(BOTH),
        P(BOTH),
        P(BOTH),
        P(BOTH),
        P(BOTH, None),
        P(BOTH, None),
        P(BOTH, None, None),
        P(BOTH, None, None),
        P("tm", None),
        P(),
    )
    out_specs = (P(BOTH, None, None), P(BOTH, None, None), P("tm", None), P())
    return jax.shard_map(shards, mesh=mesh, in_specs=in_specs, out_specs=out_specs, check_vma=False)
```

time: 952 us -> 333 us (0.35)
  blocking collectives: 547 us -> 55.2 us
  waiting for transfers between devices: 226 us -> 80.1 us
  Pallas kernels: 0 us -> 135 us
  matrix products: 59.7 us -> 14.5 us
  loops' own time: 29.2 us -> 0 us
  other arithmetic: 26.9 us -> 6.23 us
  starting transfers between devices: 19.8 us -> 8.22 us
    all_to_all x1, blocking collectives: 547 us -> 14.2 us  [shards(): held = exchange(jnp.concatenate([users_ask, items_ask], 1))]
    psum x2 -> x0, waiting for transfers between devices: 174 us -> none  [the longest x1 138 us: shards(): core_total = lax.psum(own_term, ('tm', 'rows'))]
    pallas_call x0 -> x1, Pallas kernels: none -> 135 us  [tiles_in_kernel(): pl.pallas_call(functools.partial(tile_kernel, chunk, group, steps, rank),...]
    dot_general x14 -> x5, matrix products: 59.7 us -> 14.5 us  [the longest x1 5.59 us: shards(): jnp.einsum('spq,sr->pqr', every, time_all, precision=HIGH)]
    all_gather x0 -> x1, blocking collectives: none -> 40.9 us  [shards(): time_all = lax.all_gather(time_factor, 'tm', axis=0, tiled=True)]
    another operation x1 -> x0, loops' own time: 29.2 us -> none  [shards(): lax.fori_loop(0, block_total, one_block, start_carry)]
    reduce_scatter x0 -> x1, waiting for transfers between devices: none -> 27.2 us  [shards(): lax.psum_scatter(step_sums.reshape(steps * rank * rank // 128, 128), 'row...]
    scatter-add x2 -> x0, other arithmetic: 17.4 us -> none  [the longest x1 10.3 us: one_block(): grad_left = grad_left.at[slots_user].add(grad_u)]
  transfers between devices with their start and end apart: 7 -> 4, of which waited for: 6 -> 3; matrix products, arithmetic and copies ran while one was open for 3% -> 6% of each run, Pallas kernels for 0% -> 0%
where the time goes in v1:
time: 333 us; the launch traced here: 332 us
  Pallas kernels  135 us (41%)
  waiting for transfers between devices  80.1 us (24%)
  blocking collectives  55.2 us (17%)
  local copies, waits for them, and re-layouts  18.1 us (5%)
  between operations  14.9 us (4%)
  matrix products  14.5 us (4%)
  starting transfers between devices  8.22 us (2%)
  other arithmetic  6.23 us (2%)
    pallas_call x1, Pallas kernels, tiles_in_kernel(): pl.pallas_call(functools.partial(tile_kernel, chunk, group, steps, rank),...  135 us
    all_gather x1, blocking collectives, shards(): time_all = lax.all_gather(time_factor, 'tm', axis=0, tiled=True)  40.9 us
    all_to_all x1, waiting for transfers between devices, shards(): back = exchange(found)  39.8 us
    reduce_scatter x1, waiting for transfers between devices, shards(): lax.psum_scatter(step_sums.reshape(steps * rank * rank // 128, 128), 'row...  27.2 us
    all_to_all x1, blocking collectives, shards(): held = exchange(jnp.concatenate([users_ask, items_ask], 1))  14.2 us
    all_gather x1, waiting for transfers between devices, shards(): every = lax.all_gather(own_steps, BOTH, axis=0, tiled=True)  13.1 us
  transfers between devices with their start and end apart: 4, of which 3 were waited for; matrix products, arithmetic and copies ran while one was open for 6% of the time, Pallas kernels for 0%

profile of v1, /device:TPU:0, one launch (start us, length us, event | category | flops | bytes accessed | tf_op | source)
XLA Modules:
  0.0 332.4 jit_solution(17621758030507172102)
XLA Ops:
  7.2 0.0 copy-start
  7.2 0.8 add_bitcast_fusion
  8.0 0.1 copy.34
  8.1 14.2 %all_to_all.22 = s32[32,1,2]{2,1,0:T(1,128)S(1)} all-to-all(s32[32,1,2]{2,1,0:T(1,128)S(1)} %copy.34), channel_id=1, replica_groups=mesh['tm'=8,'rows'=4] {'tm','rows'}, dimensions={0} | all-to-all | bytes 512 | tf_op jit(solution)/shard_map/all_to_all | solution.py:222
  22.3 0.1 copy.35
  22.5 0.0 copy-start.2
  22.5 1.6 gather_fusion
  24.1 1.1 bitcast_select_fusion.1
  25.2 0.6 gather_fusion.1
  25.8 0.0 copy-start.3
  25.8 0.1 bitcast_select_fusion
  26.0 1.1 copy-done.3
  27.1 1.5 pad_maximum_fusion
  28.5 3.6 %all-to-all-start.1 = ((f32[32,2,64,128]{3,2,1,0:T(8,128)}), f32[32,2,64,128]{3,2,1,0:T(8,128)}, u32[]{:S(2)}, u32[]{:S(2)}) async-start(f32[32,2,64,128]{3,2,1,0:T(8,128)} %pad_maximum_fusion), calls=%async_computation.1 | async-start | bytes 4194304 | tf_op jit(solution)/shard_map/all_to_all | solution.py:227
  32.2 5.0 %reduce-precision_convert_fusion.1 = (bf16[8,64,64]{2,0,1:T(8,128)(2,1)S(1)}, bf16[8,64,64]{2,0,1:T(8,128)(2,1)S(1)}, f32[8,64,64]{2,0,1:T(8,128)S(1)}) fusion(f32[64,64,64]{2,1,0:T(8,128)S(1)} %copy-done, f32[8,64]{1,0:T(8,128)S(1)} %copy-done.5), kind=kOutput, calls=%fused_computation.20 | convolution fusion | flops 25296896 | bytes 1312768 | tf_op jit(solution)/shard_map/pqr,sr->spq/dot_general | solution.py:230
  37.1 0.1 reduce-precision_convert_fusion
  37.2 0.1 maximum_maximum_fusion
  37.3 0.9 copy.40
  38.2 0.2 copy.38
  38.4 0.1 reshape.59
  38.5 0.2 copy.39
  38.7 0.1 reshape.60
  38.9 0.8 copy.41.c4
  40.4 0.6 pad_maximum_fusion.3.ct2
  41.0 39.8 %all-to-all-done.1 = f32[32,2,64,128]{3,2,1,0:T(8,128)} async-done(((f32[32,2,64,128]{3,2,1,0:T(8,128)}), f32[32,2,64,128]{3,2,1,0:T(8,128)}, u32[]{:S(2)}, u32[]{:S(2)}) %all-to-all-start.1) | async-done | bytes 2097184 | tf_op jit(solution)/shard_map/all_to_all | solution.py:227
  80.9 3.1 slice_bitcast_fusion
  84.0 135.1 %tiles.1 = (f32[32,64,128]{2,1,0:T(8,128)}, f32[32,64,128]{2,1,0:T(8,128)}, f32[512,128]{1,0:T(8,128)}) custom-call(s32[512]{0:T(512)} %users.1, s32[512]{0:T(512)} %items.1, s32[512]{0:T(512)} %tsteps.1, s32[1]{0:T(128)S(6)} %copy.64.count, bf16[512,128,128]{2,1,0:T(8,128)(2,1)} %values.1, f32[32,64,128]{2,1,0:T(8,128)} %get-tuple-element.26.left, ...), custom_call_target="tpu_custom_call" | custom-call | tf_op jit(solution)/shard_map/tiles/pallas_call | solution.py:128
  219.1 1.7 pad_maximum_fusion.1
  220.8 1.4 copy.42
  222.2 4.5 %all-to-all-start.2 = ((f32[32,2,64,128]{3,2,1,0:T(8,128)}), f32[32,2,64,128]{3,2,1,0:T(8,128)}, u32[]{:S(2)}, u32[]{:S(2)}) async-start(f32[32,2,64,128]{3,2,1,0:T(8,128)} %copy.42), calls=%async_computation.2 | async-start | bytes 4194304 | tf_op jit(solution)/shard_map/all_to_all | solution.py:248
  226.8 0.0 reduce-scatter.2.cloned.1.call-start
  226.8 0.1 slice_add_fusion
  227.0 0.8 reshape_reshape.3
  227.7 0.0 reduce-scatter.2.cloned.1.call-update
  227.7 0.0 all-gather.2.cloned.1.call-start
  227.8 27.2 %reduce-scatter.2.cloned.1.call-done = f32[64,128]{1,0:T(8,128)} async-done(((f32[256,128]{1,0:T(8,128)}), f32[64,128]{1,0:T(8,128)}) %reduce-scatter.2.cloned.1.call-update) | async-done | bytes 32784 | tf_op jit(solution)/shard_map/reduce_scatter | solution.py:243
  254.9 0.0 all-gather.2.cloned.1.call-update
  255.0 40.9 %all_gather.7 = f32[64,64]{1,0:T(8,128)S(1)} all-gather(f32[8,64]{1,0:T(8,128)S(1)} %copy-done.5), channel_id=1, replica_groups=mesh['tm'=8,'rows'=4] {'tm'}, dimensions={0}, use_global_device_ids=true | all-gather | bytes 18432 | tf_op jit(solution)/shard_map/all_gather | solution.py:231
  295.9 13.1 %all-gather.2.cloned.1.call-done = f32[2048,128]{1,0:T(8,128)} async-done(((f32[64,128]{1,0:T(8,128)}), f32[2048,128]{1,0:T(8,128)}) %all-gather.2.cloned.1.call-update) | async-done | bytes 1048592 | tf_op jit(solution)/shard_map/all_gather | solution.py:246
  309.0 2.7 reshape.66
  311.7 1.1 constant_dynamic-slice_fusion
  312.8 1.9 fusion.5
  314.6 5.6 %fusion.2 = f32[64,64,64]{2,1,0:T(8,128)} fusion(f32[64,64,64]{2,1,0:T(8,128)S(1)} %copy-done.1, f32[64,64]{1,0:T(8,128)S(1)} %all_gather.7), kind=kOutput, calls=%fused_computation.6 | convolution fusion | flops 201588736 | bytes 2113536 | tf_op jit(solution)/shard_map/spq,sr->pqr/dot_general | solution.py:265
  320.2 1.7 fusion.20
  321.9 1.0 convolution_multiply_fusion
  323.0 0.8 copy.48
  323.7 1.0 convolution_multiply_fusion.1
  324.8 0.8 copy.47
  (13 shorter events, 0.1 us)
Async XLA Ops:
  7.2 25.0 %copy-start = (f32[64,64,64]{2,1,0:T(8,128)S(1)}, f32[64,64,64]{2,1,0:T(8,128)}, u32[]{:S(2)}) copy-start(f32[64,64,64]{2,1,0:T(8,128)} %param.23) | copy-start | bytes 3145732
  22.5 2.7 copy-start.2
  25.8 1.2 copy-start.3
  28.5 3.6 %copy-start.5 = (f32[8,64]{1,0:T(8,128)S(1)}, f32[8,64]{1,0:T(8,128)}, u32[]{:S(2)}) copy-start(f32[8,64]{1,0:T(8,128)} %param.22) | copy-start | bytes 6148
  28.5 52.3 %all-to-all-start.1 = ((f32[32,2,64,128]{3,2,1,0:T(8,128)}), f32[32,2,64,128]{3,2,1,0:T(8,128)}, u32[]{:S(2)}, u32[]{:S(2)}) async-start(f32[32,2,64,128]{3,2,1,0:T(8,128)} %pad_maximum_fusion), calls=%async_computation.1 | async-start | bytes 4194304 | tf_op jit(solution)/shard_map/all_to_all | solution.py:227
  222.2 4.6 %copy-start.4 = (f32[512,128]{1,0:T(8,128)S(1)}, f32[512,128]{1,0:T(8,128)}, u32[]{:S(2)}) copy-start(f32[512,128]{1,0:T(8,128)} %get-tuple-element.10) | copy-start | bytes 786436
  222.2 98.0 %all-to-all-start.2 = ((f32[32,2,64,128]{3,2,1,0:T(8,128)}), f32[32,2,64,128]{3,2,1,0:T(8,128)}, u32[]{:S(2)}, u32[]{:S(2)}) async-start(f32[32,2,64,128]{3,2,1,0:T(8,128)} %copy.42), calls=%async_computation.2 | async-start | bytes 4194304 | tf_op jit(solution)/shard_map/all_to_all | solution.py:248
  226.8 28.2 %reduce-scatter.2.cloned.1.call-start = ((), (), s32[]{:S(2)}) async-start(), calls=%async_computation.4 | async-start | bytes 163840 | tf_op jit(solution)/shard_map/reduce_scatter | solution.py:243
  227.7 81.3 %all-gather.2.cloned.1.call-start = ((), (), s32[]{:S(2)}) async-start(), calls=%async_computation.5 | async-start | bytes 1081344 | tf_op jit(solution)/shard_map/all_gather | solution.py:246
  311.7 3.0 copy-start.1
Sparse Core Ops, SparseCore 0:
  230.6 24.3 reduce-scatter.1
  258.2 50.7 all-gather.1

commit v2 on v1

--- a/solution.py
+++ b/solution.py
@@ -30,25 +30,24 @@
 
 
 def tile_kernel(
-    chunk, group, steps, rank,
+    chunk, group, ahead, steps, rank,
     users, items, tsteps, count,
-    values, left, right, c4, ct2, cq,
-    out_u, out_v, out_d,
+    values, blocks, c4, ct2, cq,
+    out, out_d,
     u2, ut2, vt2, m2, psum, qsum,
 ):
-    slots = left.shape[0]
-    width = left.shape[2]
+    slots = blocks.shape[0]
+    width = blocks.shape[3]
     step = pl.program_id(0)
 
     @pl.when(step == 0)
     def prepare():
-        @pl.loop(0, slots)
-        def one_slot(k):
-            hi, lo = split(left[k])
+        def one_slot(k, carry):
+            hi, lo = split(blocks[k, 0])
             u2[k] = jnp.concatenate([hi, lo], 0)
             both = jnp.concatenate([hi.astype(jnp.float32), lo.astype(jnp.float32)], 0)
             ut2[k] = both.T.astype(jnp.bfloat16)
-            hi, lo = split(right[k])
+            hi, lo = split(blocks[k, 1])
             both = jnp.concatenate([hi.astype(jnp.float32), lo.astype(jnp.float32)], 0)
             vt2[k] = both.T.astype(jnp.bfloat16)
             mixed = mm(c4[...], jnp.concatenate([hi, hi, lo, lo], 0))
@@ -58,6 +57,9 @@
                 m2[k * steps + s, rank:2 * rank, :] = mlo[s * rank:(s + 1) * rank]
             psum[k] = jnp.zeros((steps * rank, width), jnp.float32)
             qsum[k] = jnp.zeros((width, steps * 2 * rank), jnp.float32)
+            return carry
+
+        lax.fori_loop(0, slots, one_slot, 0, unroll=2)
 
     base = step * chunk
     live = jnp.clip(count[0] - base, 0, chunk)
@@ -65,16 +67,22 @@
     @pl.loop(0, (live + group - 1) // group)
     def one_group(g):
         first = g * group
-        done = []
+        ids = []
         for k in range(group):
             t = base + first + k
-            u, v, s = users[t], items[t], tsteps[t]
+            ids.append((users[t], items[t], tsteps[t]))
+
+        def guess_of(k):
+            u, v, s = ids[k]
             m = m2[v * steps + s]
             mhi, mlo = m[:rank], m[rank:]
             ut = ut2[u]
-            guess = mm(
+            return mm(
                 jnp.concatenate([ut, ut], 1), jnp.concatenate([mhi, mhi, mlo, mlo], 0)
             )
+
+        def products_of(k, guess):
+            u, v, s = ids[k]
             resid = guess - values[first + k].astype(jnp.float32)
             resid = jnp.where(first + k < live, resid, 0.0)
             rhi, rlo = split(resid)
@@ -82,37 +90,51 @@
             vt = vt2[v]
             w = mm(jnp.concatenate([ul, ul], 1), jnp.concatenate([rhi, rlo], 0))
             z = mm(jnp.concatenate([rhi, rlo], 1), jnp.concatenate([vt, vt], 0))
-            done.append((u, v, s, w[:rank] + w[rank:], z))
-        for u, v, s, w, z in done:
+            return w[:rank] + w[rank:], z
+
+        def add_up(k, w, z):
+            u, v, s = ids[k]
             at_p = pl.ds(pl.multiple_of(s * rank, rank), rank)
             psum[v, at_p, :] += w
             at_q = pl.ds(pl.multiple_of(s * 2 * rank, 2 * rank), 2 * rank)
             qsum[u, :, at_q] += z
 
+        guesses, products = {}, {}
+        for k in range(group + ahead + 2):
+            if k < group:
+                guesses[k] = guess_of(k)
+            if 0 <= k - ahead < group:
+                products[k - ahead] = products_of(k - ahead, guesses.pop(k - ahead))
+            if 0 <= k - ahead - 2 < group:
+                add_up(k - ahead - 2, *products.pop(k - ahead - 2))
+
     @pl.when(step == pl.num_programs(0) - 1)
     def finish():
         out_d[...] = jnp.zeros(out_d.shape, jnp.float32)
 
-        @pl.loop(0, slots)
-        def one_slot(k):
+        def one_slot(k, carry):
             hi, lo = split(psum[k])
             g1 = mm(ct2[...], hi)
-            out_v[k] = g1[:rank] + g1[rank:] + mm(ct2[0:rank, :], lo)
+            out[k, 1] = g1[:rank] + g1[rank:] + mm(ct2[0:rank, :], lo)
             vt = vt2[k]
             out_d[...] += mm(
                 jnp.concatenate([hi, lo], 1), jnp.concatenate([vt, vt], 0)
             )
             qhi, qlo = split(qsum[k])
             g2 = (mm(qhi, cq[...]) + mm(qlo, cq[...])).T
-            out_u[k] = g2[:rank] + g2[rank:]
-
-
-def tiles_in_kernel(values, users, items, tsteps, count, left, right, cores):
-    slots, rank, width = left.shape
+            out[k, 0] = g2[:rank] + g2[rank:]
+            return carry
+
+        lax.fori_loop(0, slots, one_slot, 0, unroll=2)
+
+
+def tiles_in_kernel(values, users, items, tsteps, count, blocks, cores):
+    slots, unused, rank, width = blocks.shape
     steps = cores.shape[0]
     total = values.shape[0]
     chunk = 32
-    group = 8
+    group = 16
+    ahead = 4
     chi, clo = split_outside(cores)
     flat_hi, flat_lo = chi.reshape(steps * rank, rank), clo.reshape(steps * rank, rank)
     c4 = jnp.concatenate([flat_hi, flat_lo, flat_hi, flat_lo], 1)
@@ -126,12 +148,12 @@
 
     whole = pl.BlockSpec(memory_space=pltpu.VMEM)
     return pl.pallas_call(
-        functools.partial(tile_kernel, chunk, group, steps, rank),
+        functools.partial(tile_kernel, chunk, group, ahead, steps, rank),
         grid_spec=pltpu.PrefetchScalarGridSpec(
             num_scalar_prefetch=4,
             grid=(total // chunk,),
-            in_specs=[pl.BlockSpec((chunk, width, width), values_at)] + [whole] * 5,
-            out_specs=[whole] * 3,
+            in_specs=[pl.BlockSpec((chunk, width, width), values_at)] + [whole] * 4,
+            out_specs=[whole] * 2,
             scratch_shapes=[
                 pltpu.VMEM((slots, 2 * rank, width), jnp.bfloat16),
                 pltpu.VMEM((slots, width, 2 * rank), jnp.bfloat16),
@@ -142,15 +164,48 @@
             ],
         ),
         out_shape=[
-            jax.ShapeDtypeStruct((slots, rank, width), jnp.float32),
-            jax.ShapeDtypeStruct((slots, rank, width), jnp.float32),
+            jax.ShapeDtypeStruct(blocks.shape, jnp.float32),
             jax.ShapeDtypeStruct((steps * rank, 2 * rank), jnp.float32),
         ],
         compiler_params=pltpu.CompilerParams(
             dimension_semantics=("arbitrary",), vmem_limit_bytes=56 * 2**20
         ),
         name="tiles",
-    )(users, items, tsteps, count, values, left, right, c4, ct2, cq)
+    )(users, items, tsteps, count, values, blocks, c4, ct2, cq)
+
+
+def pick_kernel(held, left, right, out):
+    cap = held.shape[1] // 2
+
+    @pl.loop(0, held.shape[0])
+    def one_owner(k):
+        for c in range(cap):
+            out[k, c] = left[held[k, c]]
+            out[k, cap + c] = right[held[k, cap + c]]
+
+
+def owner_kernel(held, terms, out_left, out_right):
+    cap = held.shape[1] // 2
+    out_left[...] = jnp.zeros(out_left.shape, jnp.float32)
+    out_right[...] = jnp.zeros(out_right.shape, jnp.float32)
+
+    @pl.loop(0, held.shape[0])
+    def one_owner(k):
+        for c in range(cap):
+            out_left[held[k, c]] += user_scale * terms[k, c]
+            out_right[held[k, cap + c]] += user_scale * terms[k, cap + c]
+
+
+def plain_kernel(body, shapes, held, *arrays, name):
+    whole = pl.BlockSpec(memory_space=pltpu.VMEM)
+    return pl.pallas_call(
+        body,
+        in_specs=[pl.BlockSpec(memory_space=pltpu.SMEM)] + [whole] * len(arrays),
+        out_specs=[whole] * len(shapes),
+        out_shape=[jax.ShapeDtypeStruct(shape, jnp.float32) for shape in shapes],
+        compiler_params=pltpu.CompilerParams(vmem_limit_bytes=32 * 2**20),
+        name=name,
+    )(held, *arrays)
 
 
 def tiles_in_loop(values_all, users, items, tsteps, count, left_all, right_all, step_cores):
@@ -212,7 +267,6 @@
     cap = users_ask.shape[1]
     rank = user_factor.shape[1]
     width = user_factor.shape[2]
-    blocks_own = user_factor.shape[0]
     steps = time_factor.shape[0]
     slots = owners * cap
 
@@ -220,46 +274,46 @@
         lax.all_to_all, axis_name=BOTH, split_axis=0, concat_axis=0, tiled=True
     )
     held = exchange(jnp.concatenate([users_ask, items_ask], 1))
-    held_user, held_item = held[:, :cap], held[:, cap:]
-    found = jnp.concatenate(
-        [jnp.take(user_factor, held_user, axis=0), jnp.take(item_factor, held_item, axis=0)], 1
+    (found,) = plain_kernel(
+        pick_kernel,
+        [(owners, 2 * cap, rank, width)],
+        held,
+        user_factor,
+        item_factor,
+        name="pick",
     )
     back = exchange(found)
-    left = back[:, :cap].reshape(slots, rank, width)
-    right = back[:, cap:].reshape(slots, rank, width)
     cores = jnp.einsum("pqr,sr->spq", core, time_factor, precision=HIGH)
-    time_all = lax.all_gather(time_factor, "tm", axis=0, tiled=True)
-
-    if slots <= 32 and tile_values.shape[0] % 32 == 0:
-        part_u, part_v, twice = tiles_in_kernel(
-            tile_values, tile_users, tile_items, tile_steps, tile_count, left, right, cores
+
+    if slots <= 32 and cap == 1 and tile_values.shape[0] % 32 == 0:
+        terms, twice = tiles_in_kernel(
+            tile_values, tile_users, tile_items, tile_steps, tile_count, back, cores
         )
-        step_sums = (twice[:, :rank] + twice[:, rank:]).reshape(steps, rank, rank)
+        step_sums = twice[:, :rank] + twice[:, rank:]
     else:
+        left = back[:, :cap].reshape(slots, rank, width)
+        right = back[:, cap:].reshape(slots, rank, width)
         part_u, part_v, step_sums = tiles_in_loop(
             tile_values, tile_users, tile_items, tile_steps, tile_count, left, right, cores
         )
+        terms = jnp.concatenate(
+            [part_u.reshape(owners, cap, rank, width), part_v.reshape(owners, cap, rank, width)], 1
+        )
 
     own_steps = lax.psum_scatter(
         step_sums.reshape(steps * rank * rank // 128, 128), "rows", scatter_dimension=0, tiled=True
     )
-    every = lax.all_gather(own_steps, BOTH, axis=0, tiled=True)
-    every = every.reshape(count_tm * steps, rank, rank)
-    returned = exchange(
-        jnp.concatenate(
-            [part_u.reshape(owners, cap, rank, width), part_v.reshape(owners, cap, rank, width)], 1
-        )
-    )
-    own_ids = jnp.arange(blocks_own, dtype=jnp.int32)
-
-    def to_owner(ids, terms):
-        pick = (ids.reshape(slots)[:, None] == own_ids[None, :]).astype(jnp.float32)
-        return user_scale * jnp.einsum(
-            "nb,npi->bpi", pick, terms.reshape(slots, rank, width), precision=HIGH
-        )
-
-    grad_users = to_owner(held_user, returned[:, :cap])
-    grad_items = to_owner(held_item, returned[:, cap:])
+    share = steps // count_rows
+    own_time = lax.dynamic_slice_in_dim(time_factor, lax.axis_index("rows") * share, share, 0)
+    own_time = jnp.pad(own_time.reshape(-1), (0, 8 * 128 - share * rank)).reshape(8, 128)
+    every = lax.all_gather(jnp.concatenate([own_steps, own_time], 0), BOTH, axis=0)
+    time_all = every[:, -8:].reshape(owners, 8 * 128)[:, : share * rank]
+    time_all = time_all.reshape(count_tm * steps, rank)
+    every = every[:, :-8].reshape(count_tm * steps, rank, rank)
+    returned = exchange(terms)
+    grad_users, grad_items = plain_kernel(
+        owner_kernel, [user_factor.shape, item_factor.shape], held, returned, name="owner_sums"
+    )
     mine = lax.dynamic_slice_in_dim(every, lax.axis_index("tm") * steps, steps, 0)
     grad_time = time_scale * jnp.einsum("spq,pqr->sr", mine, core, precision=HIGH)
     grad_core = core_scale * jnp.einsum("spq,sr->pqr", every, time_all, precision=HIGH)

time: 333 us -> 247 us (0.74)
  Pallas kernels: 135 us -> 31.9 us
  blocking collectives: 55.2 us -> 14.2 us
  waiting for transfers between devices: 80.1 us -> 120 us
  starting transfers between devices: 8.22 us -> 38.8 us
  local copies, waits for them, and re-layouts: 18.1 us -> 11.8 us
    pallas_call x1 -> x3, Pallas kernels: 135 us -> 31.9 us  [the longest x1 28 us: tiles_in_kernel(): pl.pallas_call(functools.partial(tile_kernel, chunk, group, ahead, steps,...]
    all_gather x1 -> x0, blocking collectives: 40.9 us -> none  [shards(): time_all = lax.all_gather(time_factor, 'tm', axis=0, tiled=True)]
    all_gather x1, waiting for transfers between devices: 13.1 us -> 53.3 us  [shards(): lax.all_gather(jnp.concatenate([own_steps, own_time], 0), BOTH, axis=0)]
    all_to_all x1, starting transfers between devices: 4.52 us -> 34.9 us  [shards(): returned = exchange(terms)]
  transfers between devices with their start and end apart: 4 -> 4, of which waited for: 3 -> 3; matrix products, arithmetic and copies ran while one was open for 6% -> 9% of each run, Pallas kernels for 0% -> 0%
where the time goes in v2:
time: 247 us
  waiting for transfers between devices  120 us (49%)
  starting transfers between devices  38.8 us (16%)
  Pallas kernels  31.9 us (13%)
  between operations  14.8 us (6%)
  blocking collectives  14.2 us (6%)
  matrix products  12.4 us (5%)
  local copies, waits for them, and re-layouts  11.8 us (5%)
  other arithmetic  3.22 us (1%)
    all_gather x1, waiting for transfers between devices, shards(): lax.all_gather(jnp.concatenate([own_steps, own_time], 0), BOTH, axis=0)  53.3 us
    all_to_all x1, waiting for transfers between devices, shards(): back = exchange(found)  39.8 us
    all_to_all x1, starting transfers between devices, shards(): returned = exchange(terms)  34.9 us
    pallas_call x1, Pallas kernels, tiles_in_kernel(): pl.pallas_call(functools.partial(tile_kernel, chunk, group, ahead, steps,...  28 us
    reduce_scatter x1, waiting for transfers between devices, shards(): lax.psum_scatter(step_sums.reshape(steps * rank * rank // 128, 128), 'row...  26.9 us
    all_to_all x1, blocking collectives, shards(): held = exchange(jnp.concatenate([users_ask, items_ask], 1))  14.2 us
    dot_general x1, matrix products, shards(): jnp.einsum('spq,sr->pqr', every, time_all, precision=HIGH)  5.59 us
    dot_general x1, matrix products, shards(): cores = jnp.einsum('pqr,sr->spq', core, time_factor, precision=HIGH)  4.97 us
  transfers between devices with their start and end apart: 4, of which 3 were waited for; matrix products, arithmetic and copies ran while one was open for 9% of the time, Pallas kernels for 0%

profile of v2, /device:TPU:0, one launch (start us, length us, event | category | flops | bytes accessed | tf_op | source)
XLA Modules:
  0.0 247.2 jit_solution(12001369467062583195)
XLA Ops:
  7.2 0.0 copy-start
  7.2 0.8 add_bitcast_fusion
  8.0 0.1 copy.30
  8.1 14.2 %all_to_all.21 = s32[32,1,2]{2,1,0:T(1,128)S(1)} all-to-all(s32[32,1,2]{2,1,0:T(1,128)S(1)} %copy.30), channel_id=1, replica_groups=mesh['tm'=8,'rows'=4] {'tm','rows'}, dimensions={0} | all-to-all | bytes 512 | tf_op jit(solution)/shard_map/all_to_all | solution.py:276
  22.3 0.1 copy.31
  22.4 0.1 copy.37.held
  22.5 0.0 copy-start.2
  22.5 1.0 copy-done.2
  23.5 0.9 copy-done.3
  24.4 1.1 pick.1
  25.5 0.0 copy-start.1
  25.5 1.3 copy-done.1
  26.9 3.6 %all-to-all-start.1 = ((f32[32,2,64,128]{3,2,1,0:T(8,128)}), f32[32,2,64,128]{3,2,1,0:T(8,128)}, u32[]{:S(2)}, u32[]{:S(2)}) async-start(f32[32,2,64,128]{3,2,1,0:T(8,128)} %copy-done.1), calls=%async_computation.1 | async-start | bytes 4194304 | tf_op jit(solution)/shard_map/all_to_all | solution.py:285
  31.1 0.0 copy-done
  31.1 0.0 copy-done.6
  31.1 5.0 %reduce-precision_convert_fusion.1 = (bf16[8,64,64]{2,0,1:T(8,128)(2,1)S(1)}, bf16[8,64,64]{2,0,1:T(8,128)(2,1)S(1)}, f32[8,64,64]{2,0,1:T(8,128)S(1)}) fusion(f32[64,64,64]{2,1,0:T(8,128)S(1)} %copy-done, f32[8,64]{1,0:T(8,128)S(1)} %copy-done.6), kind=kOutput, calls=%fused_computation.8 | convolution fusion | flops 25296896 | bytes 1312768 | tf_op jit(solution)/shard_map/pqr,sr->spq/dot_general | solution.py:286
  36.1 0.2 copy.34
  36.3 0.1 reshape.38
  36.4 0.2 copy.33
  36.6 0.1 reshape.37
  36.8 0.8 copy.36.c4
  37.7 0.1 maximum_maximum_fusion
  37.8 0.9 copy.35
  38.7 0.7 pad_maximum_fusion.1.ct2
  39.4 39.8 %all-to-all-done.1.blocks = f32[32,2,64,128]{3,2,1,0:T(8,128)} async-done(((f32[32,2,64,128]{3,2,1,0:T(8,128)}), f32[32,2,64,128]{3,2,1,0:T(8,128)}, u32[]{:S(2)}, u32[]{:S(2)}) %all-to-all-start.1) | async-done | bytes 2097184 | tf_op jit(solution)/shard_map/all_to_all | solution.py:285
  79.2 28.0 %tiles.1 = (f32[32,2,64,128]{3,2,1,0:T(8,128)}, f32[512,128]{1,0:T(8,128)}) custom-call(s32[512]{0:T(512)} %users.1, s32[512]{0:T(512)} %items.1, s32[512]{0:T(512)} %tsteps.1, s32[1]{0:T(128)S(6)} %copy.50.count, bf16[512,128,128]{2,1,0:T(8,128)(2,1)} %values.1, f32[32,2,64,128]{3,2,1,0:T(8,128)} %all-to-all-done.1.blocks, bf16[512,256]{1,0:T(8,128)(2,1)} %copy.36.c4, ...), custom_call_target="tpu_custom_call" | custom-call | tf_op jit(solution)/shard_map/tiles/pallas_call | solution.py:150
  107.2 34.9 %all-to-all-start.2 = ((f32[32,2,64,128]{3,2,1,0:T(8,128)}), f32[32,2,64,128]{3,2,1,0:T(8,128)}, u32[]{:S(2)}, u32[]{:S(2)}) async-start(f32[32,2,64,128]{3,2,1,0:T(8,128)} %get-tuple-element.8), calls=%async_computation.2 | async-start | bytes 4194304 | tf_op jit(solution)/shard_map/all_to_all | solution.py:313
  142.1 0.0 reduce-scatter.2.cloned.1.call-start
  142.1 0.0 copy-done.5
  142.2 0.1 slice_add_fusion
  142.3 0.8 reshape.40
  143.0 0.0 reduce-scatter.2.cloned.1.call-update
  143.1 0.2 all-gather.3.cloned.1.call-start
  143.3 0.1 reshape.41
  143.4 26.9 %reduce-scatter.2.cloned.1.call-done = f32[64,128]{1,0:T(8,128)} async-done(((f32[256,128]{1,0:T(8,128)}), f32[64,128]{1,0:T(8,128)}) %reduce-scatter.2.cloned.1.call-update) | async-done | bytes 32784 | tf_op jit(solution)/shard_map/reduce_scatter | solution.py:303
  170.3 1.4 pad_maximum_fusion.2
  171.7 0.0 all-gather.3.cloned.1.call-update
  171.7 53.3 %all-gather.3.cloned.1.call-done = f32[2304,128]{1,0:T(8,128)} async-done(((f32[72,128]{1,0:T(8,128)}), f32[2304,128]{1,0:T(8,128)}) %all-gather.3.cloned.1.call-update) | async-done | bytes 1179664 | tf_op jit(solution)/shard_map/all_gather | solution.py:309
  225.0 1.3 slice.20
  226.3 0.9 slice.21
  227.2 1.7 reshape.43
  229.0 0.1 reshape.49
  229.0 1.1 constant_dynamic-slice_fusion
  230.1 1.9 fusion.5
  232.0 0.0 copy-done.4
  232.0 5.6 %fusion.2 = f32[64,64,64]{2,1,0:T(8,128)} fusion(f32[64,64,1]{1,0,2:T(8,128)S(1)} %reshape.49, f32[64,64,64]{2,1,0:T(8,128)S(1)} %copy-done.4), kind=kOutput, calls=%fused_computation.2 | convolution fusion | flops 201588736 | bytes 2113536 | tf_op jit(solution)/shard_map/spq,sr->pqr/dot_general | solution.py:319
  237.6 0.0 all-to-all-done.2.terms
  237.6 2.8 %owner_sums.1 = (f32[8,64,128]{2,1,0:T(8,128)}, f32[8,64,128]{2,1,0:T(8,128)}) custom-call(s32[32,2]{1,0:T(8,128)S(1)} %copy.37.held, f32[32,2,64,128]{3,2,1,0:T(8,128)} %all-to-all-done.2.terms), custom_call_target="tpu_custom_call" | custom-call | tf_op jit(solution)/shard_map/owner_sums/pallas_call | solution.py:201
  (10 shorter events, 0.1 us)
Async XLA Ops:
  7.2 24.0 %copy-start = (f32[64,64,64]{2,1,0:T(8,128)S(1)}, f32[64,64,64]{2,1,0:T(8,128)}, u32[]{:S(2)}) copy-start(f32[64,64,64]{2,1,0:T(8,128)} %param.21) | copy-start | bytes 3145732
  22.5 1.0 copy-start.2
  23.5 0.9 copy-start.3
  25.5 1.3 copy-start.1
  26.9 4.3 %copy-start.6 = (f32[8,64]{1,0:T(8,128)S(1)}, f32[8,64]{1,0:T(8,128)}, u32[]{:S(2)}) copy-start(f32[8,64]{1,0:T(8,128)} %param.20) | copy-start | bytes 6148
  26.9 52.4 %all-to-all-start.1 = ((f32[32,2,64,128]{3,2,1,0:T(8,128)}), f32[32,2,64,128]{3,2,1,0:T(8,128)}, u32[]{:S(2)}, u32[]{:S(2)}) async-start(f32[32,2,64,128]{3,2,1,0:T(8,128)} %copy-done.1), calls=%async_computation.1 | async-start | bytes 4194304 | tf_op jit(solution)/shard_map/all_to_all | solution.py:285
  107.2 34.9 %copy-start.5 = (f32[512,128]{1,0:T(8,128)S(1)}, f32[512,128]{1,0:T(8,128)}, u32[]{:S(2)}) copy-start(f32[512,128]{1,0:T(8,128)} %get-tuple-element.11) | copy-start | bytes 786436
  107.2 130.4 %all-to-all-start.2 = ((f32[32,2,64,128]{3,2,1,0:T(8,128)}), f32[32,2,64,128]{3,2,1,0:T(8,128)}, u32[]{:S(2)}, u32[]{:S(2)}) async-start(f32[32,2,64,128]{3,2,1,0:T(8,128)} %get-tuple-element.8), calls=%async_computation.2 | async-start | bytes 4194304 | tf_op jit(solution)/shard_map/all_to_all | solution.py:313
  142.1 28.2 %reduce-scatter.2.cloned.1.call-start = ((), (), s32[]{:S(2)}) async-start(), calls=%async_computation.4 | async-start | bytes 163840 | tf_op jit(solution)/shard_map/reduce_scatter | solution.py:303
  143.1 82.0 %all-gather.3.cloned.1.call-start = ((), (), s32[]{:S(2)}) async-start(), calls=%async_computation.5 | async-start | bytes 1216512 | tf_op jit(solution)/shard_map/all_gather | solution.py:309
  229.0 3.0 %copy-start.4 = (f32[64,64,64]{2,1,0:T(8,128)S(1)}, f32[64,64,64]{2,1,0:T(8,128)}, u32[]{:S(2)}) copy-start(f32[64,64,64]{2,1,0:T(8,128)} %reshape.43) | copy-start | bytes 3145732
Sparse Core Ops, SparseCore 0:
  145.9 24.3 reduce-scatter.1
  174.2 50.8 all-gather.2

commit v3 on v2

--- a/solution.py
+++ b/solution.py
@@ -132,7 +132,7 @@
     slots, unused, rank, width = blocks.shape
     steps = cores.shape[0]
     total = values.shape[0]
-    chunk = 32
+    chunk = 64
     group = 16
     ahead = 4
     chi, clo = split_outside(cores)
@@ -248,6 +248,12 @@
     return lax.fori_loop(0, (live_count + block_size - 1) // block_size, one_block, carry)
 
 
+def spread(x, axis, count):
+    return lax.all_to_all(
+        jnp.broadcast_to(x[None], (count,) + x.shape), axis, split_axis=0, concat_axis=0, tiled=True
+    )
+
+
 def shards(
     tile_values,
     tile_users,
@@ -285,7 +291,7 @@
     back = exchange(found)
     cores = jnp.einsum("pqr,sr->spq", core, time_factor, precision=HIGH)
 
-    if slots <= 32 and cap == 1 and tile_values.shape[0] % 32 == 0:
+    if slots <= 32 and cap == 1 and tile_values.shape[0] % 64 == 0:
         terms, twice = tiles_in_kernel(
             tile_values, tile_users, tile_items, tile_steps, tile_count, back, cores
         )
@@ -300,21 +306,26 @@
             [part_u.reshape(owners, cap, rank, width), part_v.reshape(owners, cap, rank, width)], 1
         )
 
-    own_steps = lax.psum_scatter(
-        step_sums.reshape(steps * rank * rank // 128, 128), "rows", scatter_dimension=0, tiled=True
-    )
     share = steps // count_rows
+    lanes = share * rank * rank // 128
+    own_steps = lax.all_to_all(
+        step_sums.reshape(count_rows, lanes, 128), "rows", split_axis=0, concat_axis=0, tiled=True
+    ).sum(0)
     own_time = lax.dynamic_slice_in_dim(time_factor, lax.axis_index("rows") * share, share, 0)
     own_time = jnp.pad(own_time.reshape(-1), (0, 8 * 128 - share * rank)).reshape(8, 128)
-    every = lax.all_gather(jnp.concatenate([own_steps, own_time], 0), BOTH, axis=0)
-    time_all = every[:, -8:].reshape(owners, 8 * 128)[:, : share * rank]
-    time_all = time_all.reshape(count_tm * steps, rank)
-    every = every[:, :-8].reshape(count_tm * steps, rank, rank)
+    piece = jnp.concatenate([own_steps, own_time], 0)
+    over_tm = spread(piece, "tm", count_tm)
+    terms, over_tm = lax.optimization_barrier((terms, over_tm))
     returned = exchange(terms)
+    every = spread(over_tm, "rows", count_rows)
+    time_all = every[:, :, lanes:].reshape(owners, 8 * 128)[:, : share * rank]
+    time_all = time_all.reshape(owners * share, rank)
+    mine = lax.dynamic_index_in_dim(every, lax.axis_index("tm"), 1, keepdims=False)
+    mine = mine[:, :lanes].reshape(steps, rank, rank)
+    every = every[:, :, :lanes].reshape(owners * share, rank, rank)
     grad_users, grad_items = plain_kernel(
         owner_kernel, [user_factor.shape, item_factor.shape], held, returned, name="owner_sums"
     )
-    mine = lax.dynamic_slice_in_dim(every, lax.axis_index("tm") * steps, steps, 0)
     grad_time = time_scale * jnp.einsum("spq,pqr->sr", mine, core, precision=HIGH)
     grad_core = core_scale * jnp.einsum("spq,sr->pqr", every, time_all, precision=HIGH)
     return (grad_users, grad_items, grad_time, grad_core)

time: 247 us -> 228 us (0.923)
  blocking collectives: 14.2 us -> 62.8 us
  waiting for transfers between devices: 120 us -> 77.8 us
  starting transfers between devices: 38.8 us -> 10.6 us
  between operations: 14.8 us -> 1.47 us
  Pallas kernels: 31.9 us -> 44.9 us
  local copies, waits for them, and re-layouts: 11.8 us -> 14.3 us
    all_gather x1 -> x0, waiting for transfers between devices: 53.3 us -> none  [shards(): lax.all_gather(jnp.concatenate([own_steps, own_time], 0), BOTH, axis=0)]
    all_to_all x0 -> x2, blocking collectives: none -> 48.6 us  [spread(): lax.all_to_all(jnp.broadcast_to(x[None], (count,) + x.shape), axis, split...]
    all_to_all x1, waiting for transfers between devices: 0.01 us -> 33.5 us  [shards(): returned = exchange(terms)]
    all_to_all x1, starting transfers between devices: 34.9 us -> 3.67 us  [shards(): returned = exchange(terms)]
    reduce_scatter x1 -> x0, waiting for transfers between devices: 26.9 us -> none  [shards(): lax.psum_scatter(step_sums.reshape(steps * rank * rank // 128, 128), 'row...]
    pallas_call x1, Pallas kernels: 28 us -> 41 us  [tiles_in_kernel(): pl.pallas_call(functools.partial(tile_kernel, chunk, group, ahead, steps,...]
    all_to_all x0 -> x1, waiting for transfers between devices: none -> 4.59 us  [shards(): lax.all_to_all(step_sums.reshape(count_rows, lanes, 128), 'rows', split_a...]
    reshape x3 -> x4, local copies, waits for them, and re-layouts: 2.49 us -> 5.84 us  [the longest x1 2.68 us: shards(): every = every[:, :, :lanes].reshape(owners * share, rank, rank)]
  transfers between devices with their start and end apart: 4 -> 3, of which waited for: 3 -> 3; matrix products, arithmetic and copies ran while one was open for 9% -> 10% of each run, Pallas kernels for 0% -> 0%
where the time goes in v3:
time: 228 us; the launch traced here: 227 us
  waiting for transfers between devices  77.8 us (34%)
  blocking collectives  62.8 us (28%)
  Pallas kernels  44.9 us (20%)
  local copies, waits for them, and re-layouts  14.3 us (6%)
  matrix products  12.4 us (5%)
  starting transfers between devices  10.6 us (5%)
  other arithmetic  2.88 us (1%)
    all_to_all x2, blocking collectives, spread(): lax.all_to_all(jnp.broadcast_to(x[None], (count,) + x.shape), axis, split...  48.6 us
    pallas_call x1, Pallas kernels, tiles_in_kernel(): pl.pallas_call(functools.partial(tile_kernel, chunk, group, ahead, steps,...  41 us
    all_to_all x1, waiting for transfers between devices, shards(): back = exchange(found)  39.7 us
    all_to_all x1, waiting for transfers between devices, shards(): returned = exchange(terms)  33.5 us
    all_to_all x1, blocking collectives, shards(): held = exchange(jnp.concatenate([users_ask, items_ask], 1))  14.2 us
    dot_general x1, matrix products, shards(): jnp.einsum('spq,sr->pqr', every, time_all, precision=HIGH)  5.59 us
    dot_general x1, matrix products, shards(): cores = jnp.einsum('pqr,sr->spq', core, time_factor, precision=HIGH)  4.97 us
    all_to_all x1, waiting for transfers between devices, shards(): lax.all_to_all(step_sums.reshape(count_rows, lanes, 128), 'rows', split_a...  4.59 us
  transfers between devices with their start and end apart: 3, of which 3 were waited for; matrix products, arithmetic and copies ran while one was open for 10% of the time, Pallas kernels for 0%

profile of v3, /device:TPU:0, one launch (start us, length us, event | category | flops | bytes accessed | tf_op | source)
XLA Modules:
  0.0 227.3 jit_solution(1873168591102774761)
XLA Ops:
  0.6 0.0 copy-start
  0.6 0.8 add_bitcast_fusion
  1.5 0.1 copy.29
  1.6 14.2 %all_to_all.36 = s32[32,1,2]{2,1,0:T(1,128)S(1)} all-to-all(s32[32,1,2]{2,1,0:T(1,128)S(1)} %copy.29), channel_id=1, replica_groups=mesh['tm'=8,'rows'=4] {'tm','rows'}, dimensions={0} | all-to-all | bytes 512 | tf_op jit(solution)/shard_map/all_to_all | solution.py:282
  15.8 0.1 copy.30
  15.9 0.1 copy.36.held
  16.0 0.0 copy-start.2
  16.0 1.0 copy-done.2
  16.9 0.0 copy-start.3
  16.9 0.9 copy-done.3
  17.9 1.1 pick.1
  19.0 0.0 copy-start.1
  19.0 1.3 copy-done.1
  20.3 3.6 %all-to-all-start.1 = ((f32[32,2,64,128]{3,2,1,0:T(8,128)}), f32[32,2,64,128]{3,2,1,0:T(8,128)}, u32[]{:S(2)}, u32[]{:S(2)}) async-start(f32[32,2,64,128]{3,2,1,0:T(8,128)} %copy-done.1), calls=%async_computation.1 | async-start | bytes 4194304 | tf_op jit(solution)/shard_map/all_to_all | solution.py:291
  24.6 0.0 copy-done
  24.6 0.0 copy-done.6
  24.6 5.0 %reduce-precision_convert_fusion.1 = (bf16[8,64,64]{2,0,1:T(8,128)(2,1)S(1)}, bf16[8,64,64]{2,0,1:T(8,128)(2,1)S(1)}, f32[8,64,64]{2,0,1:T(8,128)S(1)}) fusion(f32[64,64,64]{2,1,0:T(8,128)S(1)} %copy-done, f32[8,64]{1,0:T(8,128)S(1)} %copy-done.6), kind=kOutput, calls=%fused_computation.8 | convolution fusion | flops 25296896 | bytes 1312768 | tf_op jit(solution)/shard_map/pqr,sr->spq/dot_general | solution.py:292
  29.6 0.2 copy.33
  29.8 0.1 reshape.43
  29.9 0.2 copy.32
  30.1 0.1 reshape.42
  30.2 0.8 copy.35.c4
  31.1 0.1 maximum_maximum_fusion
  31.3 0.9 copy.34
  32.2 0.1 reshape.46
  32.3 0.7 pad_maximum_fusion.1.ct2
  33.0 39.7 %all-to-all-done.1.blocks = f32[32,2,64,128]{3,2,1,0:T(8,128)} async-done(((f32[32,2,64,128]{3,2,1,0:T(8,128)}), f32[32,2,64,128]{3,2,1,0:T(8,128)}, u32[]{:S(2)}, u32[]{:S(2)}) %all-to-all-start.1) | async-done | bytes 2097184 | tf_op jit(solution)/shard_map/all_to_all | solution.py:291
  72.7 41.0 %tiles.1 = (f32[32,2,64,128]{3,2,1,0:T(8,128)}, f32[512,128]{1,0:T(8,128)}) custom-call(s32[512]{0:T(512)} %users.1, s32[512]{0:T(512)} %items.1, s32[512]{0:T(512)} %tsteps.1, s32[1]{0:T(128)S(6)} %copy.48.count, bf16[512,128,128]{2,1,0:T(8,128)(2,1)} %values.1, f32[32,2,64,128]{3,2,1,0:T(8,128)} %all-to-all-done.1.blocks, bf16[512,256]{1,0:T(8,128)(2,1)} %copy.35.c4, ...), custom_call_target="tpu_custom_call" | custom-call | tf_op jit(solution)/shard_map/tiles/pallas_call | solution.py:150
  113.7 1.2 slice_add_fusion
  114.9 0.8 reshape.45
  115.6 3.3 %all-to-all-start.2 = ((f32[4,64,128]{2,1,0:T(8,128)}), f32[4,64,128]{2,1,0:T(8,128)S(1)}, u32[]{:S(2)}, u32[]{:S(2)}) async-start(f32[4,64,128]{2,1,0:T(8,128)} %reshape.45), calls=%async_computation.2 | async-start | bytes 262144 | tf_op jit(solution)/shard_map/all_to_all | solution.py:311
  119.0 4.6 %all-to-all-done.2 = f32[4,64,128]{2,1,0:T(8,128)S(1)} async-done(((f32[4,64,128]{2,1,0:T(8,128)}), f32[4,64,128]{2,1,0:T(8,128)S(1)}, u32[]{:S(2)}, u32[]{:S(2)}) %all-to-all-start.2) | async-done | bytes 131104 | tf_op jit(solution)/shard_map/all_to_all | solution.py:311
  123.6 30.3 %all_to_all.37 = f32[8,72,128]{2,1,0:T(8,128)S(1)} all-to-all(f32[8,72,128]{2,1,0:T(8,128)S(1)} %broadcast_in_dim.4), channel_id=1, replica_groups=mesh['tm'=8,'rows'=4] {'tm'}, dimensions={0} | all-to-all | bytes 589824 | tf_op jit(solution)/shard_map/all_to_all | solution.py:252
  153.9 0.1 broadcast_in_dim.5
  154.0 18.3 %all_to_all.38 = f32[4,8,72,128]{3,2,1,0:T(8,128)S(1)} all-to-all(f32[4,8,72,128]{3,2,1,0:T(8,128)S(1)} %broadcast_in_dim.5), channel_id=1, replica_groups=mesh['tm'=8,'rows'=4] {'rows'}, dimensions={0} | all-to-all | bytes 2359296 | tf_op jit(solution)/shard_map/all_to_all | solution.py:252
  172.3 3.7 %all-to-all-start.4 = ((f32[32,2,64,128]{3,2,1,0:T(8,128)}), f32[32,2,64,128]{3,2,1,0:T(8,128)}, u32[]{:S(2)}, u32[]{:S(2)}) async-start(f32[32,2,64,128]{3,2,1,0:T(8,128)} %get-tuple-element.12), calls=%async_computation.4 | async-start | bytes 4194304 | tf_op jit(solution)/shard_map/all_to_all | solution.py:319
  176.0 0.7 slice.24
  176.7 1.0 reshape.48
  177.7 0.6 slice.27
  178.3 1.4 reshape.54
  179.7 1.1 slice.25
  180.8 2.7 %reshape.49 = f32[64,64,64]{2,1,0:T(8,128)} reshape(f32[4,8,64,128]{3,2,1,0:T(8,128)} %slice.25) | data formatting | bytes 2097152 | tf_op jit(solution)/shard_map/reshape | solution.py:325
  183.5 1.8 fusion.5
  185.4 0.0 copy-done.5
  185.4 0.0 copy-done.4
  185.4 5.6 %fusion.2 = f32[64,64,64]{2,1,0:T(8,128)} fusion(f32[64,64,1]{1,0,2:T(8,128)S(1)} %copy-done.5, f32[64,64,64]{2,1,0:T(8,128)S(1)} %copy-done.4), kind=kOutput, calls=%fused_computation.2 | convolution fusion | flops 201588736 | bytes 2113536 | tf_op jit(solution)/shard_map/spq,sr->pqr/dot_general | solution.py:330
  191.0 33.5 %all-to-all-done.4.terms = f32[32,2,64,128]{3,2,1,0:T(8,128)} async-done(((f32[32,2,64,128]{3,2,1,0:T(8,128)}), f32[32,2,64,128]{3,2,1,0:T(8,128)}, u32[]{:S(2)}, u32[]{:S(2)}) %all-to-all-start.4) | async-done | bytes 2097184 | tf_op jit(solution)/shard_map/all_to_all | solution.py:319
  224.5 2.8 %owner_sums.1 = (f32[8,64,128]{2,1,0:T(8,128)}, f32[8,64,128]{2,1,0:T(8,128)}) custom-call(s32[32,2]{1,0:T(8,128)S(1)} %copy.36.held, f32[32,2,64,128]{3,2,1,0:T(8,128)} %all-to-all-done.4.terms), custom_call_target="tpu_custom_call" | custom-call | tf_op jit(solution)/shard_map/owner_sums/pallas_call | solution.py:201
  (13 shorter events, 0.2 us)
Async XLA Ops:
  0.6 24.0 %copy-start = (f32[64,64,64]{2,1,0:T(8,128)S(1)}, f32[64,64,64]{2,1,0:T(8,128)}, u32[]{:S(2)}) copy-start(f32[64,64,64]{2,1,0:T(8,128)} %param.21) | copy-start | bytes 3145732
  16.0 1.0 copy-start.2
  16.9 0.9 copy-start.3
  19.0 1.3 copy-start.1
  20.3 4.3 %copy-start.6 = (f32[8,64]{1,0:T(8,128)S(1)}, f32[8,64]{1,0:T(8,128)}, u32[]{:S(2)}) copy-start(f32[8,64]{1,0:T(8,128)} %param.20) | copy-start | bytes 6148
  20.3 52.4 %all-to-all-start.1 = ((f32[32,2,64,128]{3,2,1,0:T(8,128)}), f32[32,2,64,128]{3,2,1,0:T(8,128)}, u32[]{:S(2)}, u32[]{:S(2)}) async-start(f32[32,2,64,128]{3,2,1,0:T(8,128)} %copy-done.1), calls=%async_computation.1 | async-start | bytes 4194304 | tf_op jit(solution)/shard_map/all_to_all | solution.py:291
  115.6 7.9 %all-to-all-start.2 = ((f32[4,64,128]{2,1,0:T(8,128)}), f32[4,64,128]{2,1,0:T(8,128)S(1)}, u32[]{:S(2)}, u32[]{:S(2)}) async-start(f32[4,64,128]{2,1,0:T(8,128)} %reshape.45), calls=%async_computation.2 | async-start | bytes 262144 | tf_op jit(solution)/shard_map/all_to_all | solution.py:311
  172.3 52.2 %all-to-all-start.4 = ((f32[32,2,64,128]{3,2,1,0:T(8,128)}), f32[32,2,64,128]{3,2,1,0:T(8,128)}, u32[]{:S(2)}, u32[]{:S(2)}) async-start(f32[32,2,64,128]{3,2,1,0:T(8,128)} %get-tuple-element.12), calls=%async_computation.4 | async-start | bytes 4194304 | tf_op jit(solution)/shard_map/all_to_all | solution.py:319
  180.8 4.5 %copy-start.5 = (f32[64,64,1]{1,0,2:T(8,128)S(1)}, f32[64,64,1]{1,0,2:T(8,128)}, u32[]{:S(2)}) copy-start(f32[64,64,1]{1,0,2:T(8,128)} %reshape.54) | copy-start | bytes 49156
  183.5 1.9 copy-start.4

commit v4 on v3

--- a/solution.py
+++ b/solution.py
@@ -33,7 +33,7 @@
     chunk, group, ahead, steps, rank,
     users, items, tsteps, count,
     values, blocks, c4, ct2, cq,
-    out, out_d,
+    out_u, out_v, out_d,
     u2, ut2, vt2, m2, psum, qsum,
 ):
     slots = blocks.shape[0]
@@ -115,14 +115,14 @@
         def one_slot(k, carry):
             hi, lo = split(psum[k])
             g1 = mm(ct2[...], hi)
-            out[k, 1] = g1[:rank] + g1[rank:] + mm(ct2[0:rank, :], lo)
+            out_v[k, 0] = g1[:rank] + g1[rank:] + mm(ct2[0:rank, :], lo)
             vt = vt2[k]
             out_d[...] += mm(
                 jnp.concatenate([hi, lo], 1), jnp.concatenate([vt, vt], 0)
             )
             qhi, qlo = split(qsum[k])
             g2 = (mm(qhi, cq[...]) + mm(qlo, cq[...])).T
-            out[k, 0] = g2[:rank] + g2[rank:]
+            out_u[k, 0] = g2[:rank] + g2[rank:]
             return carry
 
         lax.fori_loop(0, slots, one_slot, 0, unroll=2)
@@ -153,7 +153,7 @@
             num_scalar_prefetch=4,
             grid=(total // chunk,),
             in_specs=[pl.BlockSpec((chunk, width, width), values_at)] + [whole] * 4,
-            out_specs=[whole] * 2,
+            out_specs=[whole] * 3,
             scratch_shapes=[
                 pltpu.VMEM((slots, 2 * rank, width), jnp.bfloat16),
                 pltpu.VMEM((slots, width, 2 * rank), jnp.bfloat16),
@@ -164,7 +164,8 @@
             ],
         ),
         out_shape=[
-            jax.ShapeDtypeStruct(blocks.shape, jnp.float32),
+            jax.ShapeDtypeStruct((slots, 1, rank, width), jnp.float32),
+            jax.ShapeDtypeStruct((slots, 1, rank, width), jnp.float32),
             jax.ShapeDtypeStruct((steps * rank, 2 * rank), jnp.float32),
         ],
         compiler_params=pltpu.CompilerParams(
@@ -184,7 +185,7 @@
             out[k, cap + c] = right[held[k, cap + c]]
 
 
-def owner_kernel(held, terms, out_left, out_right):
+def owner_kernel(held, terms_u, terms_v, out_left, out_right):
     cap = held.shape[1] // 2
     out_left[...] = jnp.zeros(out_left.shape, jnp.float32)
     out_right[...] = jnp.zeros(out_right.shape, jnp.float32)
@@ -192,8 +193,8 @@
     @pl.loop(0, held.shape[0])
     def one_owner(k):
         for c in range(cap):
-            out_left[held[k, c]] += user_scale * terms[k, c]
-            out_right[held[k, cap + c]] += user_scale * terms[k, cap + c]
+            out_left[held[k, c]] += user_scale * terms_u[k, c]
+            out_right[held[k, cap + c]] += user_scale * terms_v[k, c]
 
 
 def plain_kernel(body, shapes, held, *arrays, name):
@@ -292,7 +293,7 @@
     cores = jnp.einsum("pqr,sr->spq", core, time_factor, precision=HIGH)
 
     if slots <= 32 and cap == 1 and tile_values.shape[0] % 64 == 0:
-        terms, twice = tiles_in_kernel(
+        terms_u, terms_v, twice = tiles_in_kernel(
             tile_values, tile_users, tile_items, tile_steps, tile_count, back, cores
         )
         step_sums = twice[:, :rank] + twice[:, rank:]
@@ -302,10 +303,10 @@
         part_u, part_v, step_sums = tiles_in_loop(
             tile_values, tile_users, tile_items, tile_steps, tile_count, left, right, cores
         )
-        terms = jnp.concatenate(
-            [part_u.reshape(owners, cap, rank, width), part_v.reshape(owners, cap, rank, width)], 1
-        )
-
+        terms_u = part_u.reshape(owners, cap, rank, width)
+        terms_v = part_v.reshape(owners, cap, rank, width)
+
+    back_u = exchange(terms_u)
     share = steps // count_rows
     lanes = share * rank * rank // 128
     own_steps = lax.all_to_all(
@@ -315,8 +316,8 @@
     own_time = jnp.pad(own_time.reshape(-1), (0, 8 * 128 - share * rank)).reshape(8, 128)
     piece = jnp.concatenate([own_steps, own_time], 0)
     over_tm = spread(piece, "tm", count_tm)
-    terms, over_tm = lax.optimization_barrier((terms, over_tm))
-    returned = exchange(terms)
+    terms_v, over_tm = lax.optimization_barrier((terms_v, over_tm))
+    back_v = exchange(terms_v)
     every = spread(over_tm, "rows", count_rows)
     time_all = every[:, :, lanes:].reshape(owners, 8 * 128)[:, : share * rank]
     time_all = time_all.reshape(owners * share, rank)
@@ -324,7 +325,7 @@
     mine = mine[:, :lanes].reshape(steps, rank, rank)
     every = every[:, :, :lanes].reshape(owners * share, rank, rank)
     grad_users, grad_items = plain_kernel(
-        owner_kernel, [user_factor.shape, item_factor.shape], held, returned, name="owner_sums"
+        owner_kernel, [user_factor.shape, item_factor.shape], held, back_u, back_v, name="owner_sums"
     )
     grad_time = time_scale * jnp.einsum("spq,pqr->sr", mine, core, precision=HIGH)
     grad_core = core_scale * jnp.einsum("spq,sr->pqr", every, time_all, precision=HIGH)

time: 228 us -> 235 us (1.031)
  waiting for transfers between devices: 77.8 us -> 55.8 us
  Pallas kernels: 44.9 us -> 62.3 us
  blocking collectives: 62.8 us -> 74.9 us
    all_to_all x0 -> x1, blocking collectives: none -> 28 us  [shards(): back_u = exchange(terms_u)]
    all_to_all x1, waiting for transfers between devices: 33.5 us -> 11.5 us  [shards(): back_v = exchange(terms_v)]
    pallas_call x1, Pallas kernels: 41 us -> 58.8 us  [tiles_in_kernel(): pl.pallas_call(functools.partial(tile_kernel, chunk, group, ahead, steps,...]
    all_to_all x2, blocking collectives: 48.6 us -> 32.7 us  [spread(): lax.all_to_all(jnp.broadcast_to(x[None], (count,) + x.shape), axis, split...]
where the time goes in v4:
time: 235 us
  blocking collectives  74.9 us (32%)
  Pallas kernels  62.3 us (27%)
  waiting for transfers between devices  55.8 us (24%)
  local copies, waits for them, and re-layouts  13.9 us (6%)
  matrix products  12.4 us (5%)
  starting transfers between devices  10.9 us (5%)
  other arithmetic  2.87 us (1%)
    pallas_call x1, Pallas kernels, tiles_in_kernel(): pl.pallas_call(functools.partial(tile_kernel, chunk, group, ahead, steps,...  58.8 us
    all_to_all x1, waiting for transfers between devices, shards(): back = exchange(found)  39.7 us
    all_to_all x2, blocking collectives, spread(): lax.all_to_all(jnp.broadcast_to(x[None], (count,) + x.shape), axis, split...  32.7 us
    all_to_all x1, blocking collectives, shards(): back_u = exchange(terms_u)  28 us
    all_to_all x1, blocking collectives, shards(): held = exchange(jnp.concatenate([users_ask, items_ask], 1))  14.2 us
    all_to_all x1, waiting for transfers between devices, shards(): back_v = exchange(terms_v)  11.5 us
    dot_general x1, matrix products, shards(): jnp.einsum('spq,sr->pqr', every, time_all, precision=HIGH)  5.59 us
    dot_general x1, matrix products, shards(): cores = jnp.einsum('pqr,sr->spq', core, time_factor, precision=HIGH)  4.97 us
  transfers between devices with their start and end apart: 3, of which 3 were waited for; matrix products, arithmetic and copies ran while one was open for 10% of the time, Pallas kernels for 0%

profile of v4, /device:TPU:0, one launch (start us, length us, event | category | flops | bytes accessed | tf_op | source)
XLA Modules:
  0.0 234.5 jit_solution(12736513504076157755)
XLA Ops:
  0.6 0.0 copy-start
  0.6 0.8 add_bitcast_fusion
  1.5 0.1 copy.29
  1.6 14.2 %all_to_all.41 = s32[32,1,2]{2,1,0:T(1,128)S(1)} all-to-all(s32[32,1,2]{2,1,0:T(1,128)S(1)} %copy.29), channel_id=1, replica_groups=mesh['tm'=8,'rows'=4] {'tm','rows'}, dimensions={0} | all-to-all | bytes 512 | tf_op jit(solution)/shard_map/all_to_all | solution.py:283
  15.8 0.1 copy.30
  15.9 0.1 copy.36.held
  16.0 1.0 copy-done.2
  16.9 0.9 copy-done.3
  17.9 1.1 pick.1
  19.0 0.0 copy-start.1
  19.0 1.3 copy-done.1
  20.3 3.6 %all-to-all-start.1 = ((f32[32,2,64,128]{3,2,1,0:T(8,128)}), f32[32,2,64,128]{3,2,1,0:T(8,128)}, u32[]{:S(2)}, u32[]{:S(2)}) async-start(f32[32,2,64,128]{3,2,1,0:T(8,128)} %copy-done.1), calls=%async_computation.1 | async-start | bytes 4194304 | tf_op jit(solution)/shard_map/all_to_all | solution.py:292
  24.6 0.0 copy-done
  24.6 0.0 copy-done.6
  24.6 5.0 %reduce-precision_convert_fusion.1 = (bf16[8,64,64]{2,0,1:T(8,128)(2,1)S(1)}, bf16[8,64,64]{2,0,1:T(8,128)(2,1)S(1)}, f32[8,64,64]{2,0,1:T(8,128)S(1)}) fusion(f32[64,64,64]{2,1,0:T(8,128)S(1)} %copy-done, f32[8,64]{1,0:T(8,128)S(1)} %copy-done.6), kind=kOutput, calls=%fused_computation.8 | convolution fusion | flops 25296896 | bytes 1312768 | tf_op jit(solution)/shard_map/pqr,sr->spq/dot_general | solution.py:293
  29.6 0.2 copy.33
  29.8 0.1 reshape.43
  29.9 0.2 copy.32
  30.1 0.1 reshape.42
  30.2 0.8 copy.35.c4
  31.1 0.1 maximum_maximum_fusion
  31.3 0.9 copy.34
  32.2 0.1 reshape.46
  32.3 0.7 pad_maximum_fusion.1.ct2
  32.9 39.7 %all-to-all-done.1.blocks = f32[32,2,64,128]{3,2,1,0:T(8,128)} async-done(((f32[32,2,64,128]{3,2,1,0:T(8,128)}), f32[32,2,64,128]{3,2,1,0:T(8,128)}, u32[]{:S(2)}, u32[]{:S(2)}) %all-to-all-start.1) | async-done | bytes 2097184 | tf_op jit(solution)/shard_map/all_to_all | solution.py:292
  72.7 58.8 %tiles.1 = (f32[32,1,64,128]{3,2,1,0:T(8,128)}, f32[32,1,64,128]{3,2,1,0:T(8,128)}, f32[512,128]{1,0:T(8,128)}) custom-call(s32[512]{0:T(512)} %users.1, s32[512]{0:T(512)} %items.1, s32[512]{0:T(512)} %tsteps.1, s32[1]{0:T(128)S(6)} %copy.48.count, bf16[512,128,128]{2,1,0:T(8,128)(2,1)} %values.1, f32[32,2,64,128]{3,2,1,0:T(8,128)} %all-to-all-done.1.blocks, ...), custom_call_target="tpu_custom_call" | custom-call | tf_op jit(solution)/shard_map/tiles/pallas_call | solution.py:150
  131.5 1.2 slice_add_fusion
  132.6 0.8 reshape.45
  133.4 3.3 %all-to-all-start.3 = ((f32[4,64,128]{2,1,0:T(8,128)}), f32[4,64,128]{2,1,0:T(8,128)S(1)}, u32[]{:S(2)}, u32[]{:S(2)}) async-start(f32[4,64,128]{2,1,0:T(8,128)} %reshape.45), calls=%async_computation.3 | async-start | bytes 262144 | tf_op jit(solution)/shard_map/all_to_all | solution.py:312
  136.7 4.6 %all-to-all-done.3 = f32[4,64,128]{2,1,0:T(8,128)S(1)} async-done(((f32[4,64,128]{2,1,0:T(8,128)}), f32[4,64,128]{2,1,0:T(8,128)S(1)}, u32[]{:S(2)}, u32[]{:S(2)}) %all-to-all-start.3) | async-done | bytes 131104 | tf_op jit(solution)/shard_map/all_to_all | solution.py:312
  141.4 0.0 copy-start.5
  141.4 13.7 %all_to_all.42 = f32[8,72,128]{2,1,0:T(8,128)S(1)} all-to-all(f32[8,72,128]{2,1,0:T(8,128)S(1)} %broadcast_in_dim.4), channel_id=1, replica_groups=mesh['tm'=8,'rows'=4] {'tm'}, dimensions={0} | all-to-all | bytes 589824 | tf_op jit(solution)/shard_map/all_to_all | solution.py:253
  155.1 0.1 broadcast_in_dim.5
  155.1 19.0 %all_to_all.43 = f32[4,8,72,128]{3,2,1,0:T(8,128)} all-to-all(f32[4,8,72,128]{3,2,1,0:T(8,128)S(1)} %broadcast_in_dim.5), channel_id=1, replica_groups=mesh['tm'=8,'rows'=4] {'rows'}, dimensions={0} | all-to-all | bytes 2359296 | tf_op jit(solution)/shard_map/all_to_all | solution.py:253
  174.2 0.0 copy-done.5
  174.2 28.0 %all_to_all.44.terms_u = f32[32,1,64,128]{3,2,1,0:T(8,128)S(1)} all-to-all(f32[32,1,64,128]{3,2,1,0:T(8,128)S(1)} %copy-done.5), channel_id=1, replica_groups=mesh['tm'=8,'rows'=4] {'tm','rows'}, dimensions={0} | all-to-all | bytes 2097152 | tf_op jit(solution)/shard_map/all_to_all | solution.py:309
  202.2 3.9 %all-to-all-start.5 = ((f32[32,1,64,128]{3,2,1,0:T(8,128)}), f32[32,1,64,128]{3,2,1,0:T(8,128)}, u32[]{:S(2)}, u32[]{:S(2)}) async-start(f32[32,1,64,128]{3,2,1,0:T(8,128)} %get-tuple-element.14), calls=%async_computation.5 | async-start | bytes 2097152 | tf_op jit(solution)/shard_map/all_to_all | solution.py:320
  206.1 0.9 dynamic-slice_bitcast_fusion
  207.1 0.1 reshape.48
  207.2 0.9 slice_bitcast_fusion
  208.1 0.1 reshape.54
  208.2 2.3 slice.25
  210.5 2.7 %reshape.49 = f32[64,64,64]{2,1,0:T(8,128)} reshape(f32[4,8,64,128]{3,2,1,0:T(8,128)} %slice.25) | data formatting | bytes 2097152 | tf_op jit(solution)/shard_map/reshape | solution.py:326
  213.2 1.8 fusion.5
  215.0 0.0 copy-done.4
  215.0 5.6 %fusion.2 = f32[64,64,64]{2,1,0:T(8,128)} fusion(f32[64,64,1]{1,0,2:T(8,128)S(1)} %reshape.54, f32[64,64,64]{2,1,0:T(8,128)S(1)} %copy-done.4), kind=kOutput, calls=%fused_computation.2 | convolution fusion | flops 201588736 | bytes 2113536 | tf_op jit(solution)/shard_map/spq,sr->pqr/dot_general | solution.py:331
  220.6 11.5 %all-to-all-done.5.terms_v = f32[32,1,64,128]{3,2,1,0:T(8,128)} async-done(((f32[32,1,64,128]{3,2,1,0:T(8,128)}), f32[32,1,64,128]{3,2,1,0:T(8,128)}, u32[]{:S(2)}, u32[]{:S(2)}) %all-to-all-start.5) | async-done | bytes 1048608 | tf_op jit(solution)/shard_map/all_to_all | solution.py:320
  232.1 2.4 %owner_sums.1 = (f32[8,64,128]{2,1,0:T(8,128)}, f32[8,64,128]{2,1,0:T(8,128)}) custom-call(s32[32,2]{1,0:T(8,128)S(1)} %copy.36.held, f32[32,1,64,128]{3,2,1,0:T(8,128)S(1)} %all_to_all.44.terms_u, f32[32,1,64,128]{3,2,1,0:T(8,128)} %all-to-all-done.5.terms_v), custom_call_target="tpu_custom_call" | custom-call | tf_op jit(solution)/shard_map/owner_sums/pallas_call | solution.py:202
  (14 shorter events, 0.2 us)
Async XLA Ops:
  0.6 24.0 %copy-start = (f32[64,64,64]{2,1,0:T(8,128)S(1)}, f32[64,64,64]{2,1,0:T(8,128)}, u32[]{:S(2)}) copy-start(f32[64,64,64]{2,1,0:T(8,128)} %param.21) | copy-start | bytes 3145732
  16.0 1.0 copy-start.2
  16.9 0.9 copy-start.3
  19.0 1.3 copy-start.1
  20.3 4.3 %copy-start.6 = (f32[8,64]{1,0:T(8,128)S(1)}, f32[8,64]{1,0:T(8,128)}, u32[]{:S(2)}) copy-start(f32[8,64]{1,0:T(8,128)} %param.20) | copy-start | bytes 6148
  20.3 52.3 %all-to-all-start.1 = ((f32[32,2,64,128]{3,2,1,0:T(8,128)}), f32[32,2,64,128]{3,2,1,0:T(8,128)}, u32[]{:S(2)}, u32[]{:S(2)}) async-start(f32[32,2,64,128]{3,2,1,0:T(8,128)} %copy-done.1), calls=%async_computation.1 | async-start | bytes 4194304 | tf_op jit(solution)/shard_map/all_to_all | solution.py:292
  133.4 7.9 %all-to-all-start.3 = ((f32[4,64,128]{2,1,0:T(8,128)}), f32[4,64,128]{2,1,0:T(8,128)S(1)}, u32[]{:S(2)}, u32[]{:S(2)}) async-start(f32[4,64,128]{2,1,0:T(8,128)} %reshape.45), calls=%async_computation.3 | async-start | bytes 262144 | tf_op jit(solution)/shard_map/all_to_all | solution.py:312
  141.4 32.8 %copy-start.5 = (f32[32,1,64,128]{3,2,1,0:T(8,128)S(1)}, f32[32,1,64,128]{3,2,1,0:T(8,128)}, u32[]{:S(2)}) copy-start(f32[32,1,64,128]{3,2,1,0:T(8,128)} %get-tuple-element.11) | copy-start | bytes 3145732
  202.2 30.0 %all-to-all-start.5 = ((f32[32,1,64,128]{3,2,1,0:T(8,128)}), f32[32,1,64,128]{3,2,1,0:T(8,128)}, u32[]{:S(2)}, u32[]{:S(2)}) async-start(f32[32,1,64,128]{3,2,1,0:T(8,128)} %get-tuple-element.14), calls=%async_computation.5 | async-start | bytes 2097152 | tf_op jit(solution)/shard_map/all_to_all | solution.py:320
  213.2 1.9 copy-start.4

commit v5 on v3

--- a/solution.py
+++ b/solution.py
@@ -315,7 +315,6 @@
     own_time = jnp.pad(own_time.reshape(-1), (0, 8 * 128 - share * rank)).reshape(8, 128)
     piece = jnp.concatenate([own_steps, own_time], 0)
     over_tm = spread(piece, "tm", count_tm)
-    terms, over_tm = lax.optimization_barrier((terms, over_tm))
     returned = exchange(terms)
     every = spread(over_tm, "rows", count_rows)
     time_all = every[:, :, lanes:].reshape(owners, 8 * 128)[:, : share * rank]

time: 228 us -> 228 us (level)
  Pallas kernels: 44.9 us -> 62.6 us
  blocking collectives: 62.8 us -> 45.2 us
    pallas_call x1, Pallas kernels: 41 us -> 58.7 us  [tiles_in_kernel(): pl.pallas_call(functools.partial(tile_kernel, chunk, group, ahead, steps,...]
    all_to_all x2, blocking collectives: 48.6 us -> 30.9 us  [spread(): lax.all_to_all(jnp.broadcast_to(x[None], (count,) + x.shape), axis, split...]
where the time goes in v5:
time: 228 us; the launch traced here: 227 us
  waiting for transfers between devices  77.8 us (34%)
  Pallas kernels  62.6 us (27%)
  blocking collectives  45.2 us (20%)
  local copies, waits for them, and re-layouts  14.3 us (6%)
  matrix products  12.4 us (5%)
  starting transfers between devices  10.6 us (5%)
  other arithmetic  2.88 us (1%)
    pallas_call x1, Pallas kernels, tiles_in_kernel(): pl.pallas_call(functools.partial(tile_kernel, chunk, group, ahead, steps,...  58.7 us
    all_to_all x1, waiting for transfers between devices, shards(): back = exchange(found)  39.7 us
    all_to_all x1, waiting for transfers between devices, shards(): returned = exchange(terms)  33.5 us
    all_to_all x2, blocking collectives, spread(): lax.all_to_all(jnp.broadcast_to(x[None], (count,) + x.shape), axis, split...  30.9 us
    all_to_all x1, blocking collectives, shards(): held = exchange(jnp.concatenate([users_ask, items_ask], 1))  14.2 us
    dot_general x1, matrix products, shards(): jnp.einsum('spq,sr->pqr', every, time_all, precision=HIGH)  5.59 us
    dot_general x1, matrix products, shards(): cores = jnp.einsum('pqr,sr->spq', core, time_factor, precision=HIGH)  4.97 us
    all_to_all x1, waiting for transfers between devices, shards(): lax.all_to_all(step_sums.reshape(count_rows, lanes, 128), 'rows', split_a...  4.59 us
  transfers between devices with their start and end apart: 3, of which 3 were waited for; matrix products, arithmetic and copies ran while one was open for 10% of the time, Pallas kernels for 0%

profile of v5, /device:TPU:0, one launch (start us, length us, event | category | flops | bytes accessed | tf_op | source)
XLA Modules:
  0.0 227.3 jit_solution(15186605663582461704)
XLA Ops:
  0.6 0.0 copy-start
  0.6 0.8 add_bitcast_fusion
  1.5 0.1 copy.29
  1.6 14.2 %all_to_all.36 = s32[32,1,2]{2,1,0:T(1,128)S(1)} all-to-all(s32[32,1,2]{2,1,0:T(1,128)S(1)} %copy.29), channel_id=1, replica_groups=mesh['tm'=8,'rows'=4] {'tm','rows'}, dimensions={0} | all-to-all | bytes 512 | tf_op jit(solution)/shard_map/all_to_all | solution.py:282
  15.8 0.1 copy.30
  15.9 0.1 copy.36.held
  16.0 0.0 copy-start.2
  16.0 1.0 copy-done.2
  16.9 0.0 copy-start.3
  16.9 0.9 copy-done.3
  17.9 1.1 pick.1
  19.0 0.0 copy-start.1
  19.0 1.3 copy-done.1
  20.3 3.6 %all-to-all-start.1 = ((f32[32,2,64,128]{3,2,1,0:T(8,128)}), f32[32,2,64,128]{3,2,1,0:T(8,128)}, u32[]{:S(2)}, u32[]{:S(2)}) async-start(f32[32,2,64,128]{3,2,1,0:T(8,128)} %copy-done.1), calls=%async_computation.1 | async-start | bytes 4194304 | tf_op jit(solution)/shard_map/all_to_all | solution.py:291
  24.6 0.0 copy-done
  24.6 0.0 copy-done.6
  24.6 5.0 %reduce-precision_convert_fusion.1 = (bf16[8,64,64]{2,0,1:T(8,128)(2,1)S(1)}, bf16[8,64,64]{2,0,1:T(8,128)(2,1)S(1)}, f32[8,64,64]{2,0,1:T(8,128)S(1)}) fusion(f32[64,64,64]{2,1,0:T(8,128)S(1)} %copy-done, f32[8,64]{1,0:T(8,128)S(1)} %copy-done.6), kind=kOutput, calls=%fused_computation.8 | convolution fusion | flops 25296896 | bytes 1312768 | tf_op jit(solution)/shard_map/pqr,sr->spq/dot_general | solution.py:292
  29.6 0.2 copy.33
  29.8 0.1 reshape.43
  29.9 0.2 copy.32
  30.1 0.1 reshape.42
  30.2 0.8 copy.35.c4
  31.1 0.1 maximum_maximum_fusion
  31.3 0.9 copy.34
  32.2 0.1 reshape.46
  32.3 0.7 pad_maximum_fusion.1.ct2
  33.0 39.7 %all-to-all-done.1.blocks = f32[32,2,64,128]{3,2,1,0:T(8,128)} async-done(((f32[32,2,64,128]{3,2,1,0:T(8,128)}), f32[32,2,64,128]{3,2,1,0:T(8,128)}, u32[]{:S(2)}, u32[]{:S(2)}) %all-to-all-start.1) | async-done | bytes 2097184 | tf_op jit(solution)/shard_map/all_to_all | solution.py:291
  72.7 58.7 %tiles.1 = (f32[32,2,64,128]{3,2,1,0:T(8,128)}, f32[512,128]{1,0:T(8,128)}) custom-call(s32[512]{0:T(512)} %users.1, s32[512]{0:T(512)} %items.1, s32[512]{0:T(512)} %tsteps.1, s32[1]{0:T(128)S(6)} %copy.48.count, bf16[512,128,128]{2,1,0:T(8,128)(2,1)} %values.1, f32[32,2,64,128]{3,2,1,0:T(8,128)} %all-to-all-done.1.blocks, bf16[512,256]{1,0:T(8,128)(2,1)} %copy.35.c4, ...), custom_call_target="tpu_custom_call" | custom-call | tf_op jit(solution)/shard_map/tiles/pallas_call | solution.py:150
  131.4 1.2 slice_add_fusion
  132.6 0.8 reshape.45
  133.3 3.3 %all-to-all-start.3 = ((f32[4,64,128]{2,1,0:T(8,128)}), f32[4,64,128]{2,1,0:T(8,128)S(1)}, u32[]{:S(2)}, u32[]{:S(2)}) async-start(f32[4,64,128]{2,1,0:T(8,128)} %reshape.45), calls=%async_computation.3 | async-start | bytes 262144 | tf_op jit(solution)/shard_map/all_to_all | solution.py:311
  136.7 4.6 %all-to-all-done.3 = f32[4,64,128]{2,1,0:T(8,128)S(1)} async-done(((f32[4,64,128]{2,1,0:T(8,128)}), f32[4,64,128]{2,1,0:T(8,128)S(1)}, u32[]{:S(2)}, u32[]{:S(2)}) %all-to-all-start.3) | async-done | bytes 131104 | tf_op jit(solution)/shard_map/all_to_all | solution.py:311
  141.3 12.6 %all_to_all.37 = f32[8,72,128]{2,1,0:T(8,128)S(1)} all-to-all(f32[8,72,128]{2,1,0:T(8,128)S(1)} %broadcast_in_dim.4), channel_id=1, replica_groups=mesh['tm'=8,'rows'=4] {'tm'}, dimensions={0} | all-to-all | bytes 589824 | tf_op jit(solution)/shard_map/all_to_all | solution.py:252
  154.0 0.1 broadcast_in_dim.5
  154.0 18.3 %all_to_all.38 = f32[4,8,72,128]{3,2,1,0:T(8,128)S(1)} all-to-all(f32[4,8,72,128]{3,2,1,0:T(8,128)S(1)} %broadcast_in_dim.5), channel_id=1, replica_groups=mesh['tm'=8,'rows'=4] {'rows'}, dimensions={0} | all-to-all | bytes 2359296 | tf_op jit(solution)/shard_map/all_to_all | solution.py:252
  172.3 3.7 %all-to-all-start.2 = ((f32[32,2,64,128]{3,2,1,0:T(8,128)}), f32[32,2,64,128]{3,2,1,0:T(8,128)}, u32[]{:S(2)}, u32[]{:S(2)}) async-start(f32[32,2,64,128]{3,2,1,0:T(8,128)} %get-tuple-element.8), calls=%async_computation.2 | async-start | bytes 4194304 | tf_op jit(solution)/shard_map/all_to_all | solution.py:318
  176.0 0.7 slice.24
  176.7 1.0 reshape.48
  177.8 0.6 slice.27
  178.4 1.4 reshape.54
  179.8 1.1 slice.25
  180.9 2.7 %reshape.49 = f32[64,64,64]{2,1,0:T(8,128)} reshape(f32[4,8,64,128]{3,2,1,0:T(8,128)} %slice.25) | data formatting | bytes 2097152 | tf_op jit(solution)/shard_map/reshape | solution.py:324
  183.6 1.8 fusion.5
  185.4 0.0 copy-done.5
  185.4 0.0 copy-done.4
  185.4 5.6 %fusion.2 = f32[64,64,64]{2,1,0:T(8,128)} fusion(f32[64,64,1]{1,0,2:T(8,128)S(1)} %copy-done.5, f32[64,64,64]{2,1,0:T(8,128)S(1)} %copy-done.4), kind=kOutput, calls=%fused_computation.2 | convolution fusion | flops 201588736 | bytes 2113536 | tf_op jit(solution)/shard_map/spq,sr->pqr/dot_general | solution.py:329
  191.0 33.5 %all-to-all-done.2.terms = f32[32,2,64,128]{3,2,1,0:T(8,128)} async-done(((f32[32,2,64,128]{3,2,1,0:T(8,128)}), f32[32,2,64,128]{3,2,1,0:T(8,128)}, u32[]{:S(2)}, u32[]{:S(2)}) %all-to-all-start.2) | async-done | bytes 2097184 | tf_op jit(solution)/shard_map/all_to_all | solution.py:318
  224.6 2.8 %owner_sums.1 = (f32[8,64,128]{2,1,0:T(8,128)}, f32[8,64,128]{2,1,0:T(8,128)}) custom-call(s32[32,2]{1,0:T(8,128)S(1)} %copy.36.held, f32[32,2,64,128]{3,2,1,0:T(8,128)} %all-to-all-done.2.terms), custom_call_target="tpu_custom_call" | custom-call | tf_op jit(solution)/shard_map/owner_sums/pallas_call | solution.py:201
  (13 shorter events, 0.2 us)
Async XLA Ops:
  0.6 24.0 %copy-start = (f32[64,64,64]{2,1,0:T(8,128)S(1)}, f32[64,64,64]{2,1,0:T(8,128)}, u32[]{:S(2)}) copy-start(f32[64,64,64]{2,1,0:T(8,128)} %param.21) | copy-start | bytes 3145732
  16.0 1.0 copy-start.2
  16.9 0.9 copy-start.3
  19.0 1.3 copy-start.1
  20.3 4.3 %copy-start.6 = (f32[8,64]{1,0:T(8,128)S(1)}, f32[8,64]{1,0:T(8,128)}, u32[]{:S(2)}) copy-start(f32[8,64]{1,0:T(8,128)} %param.20) | copy-start | bytes 6148
  20.3 52.4 %all-to-all-start.1 = ((f32[32,2,64,128]{3,2,1,0:T(8,128)}), f32[32,2,64,128]{3,2,1,0:T(8,128)}, u32[]{:S(2)}, u32[]{:S(2)}) async-start(f32[32,2,64,128]{3,2,1,0:T(8,128)} %copy-done.1), calls=%async_computation.1 | async-start | bytes 4194304 | tf_op jit(solution)/shard_map/all_to_all | solution.py:291
  133.3 7.9 %all-to-all-start.3 = ((f32[4,64,128]{2,1,0:T(8,128)}), f32[4,64,128]{2,1,0:T(8,128)S(1)}, u32[]{:S(2)}, u32[]{:S(2)}) async-start(f32[4,64,128]{2,1,0:T(8,128)} %reshape.45), calls=%async_computation.3 | async-start | bytes 262144 | tf_op jit(solution)/shard_map/all_to_all | solution.py:311
  172.3 52.2 %all-to-all-start.2 = ((f32[32,2,64,128]{3,2,1,0:T(8,128)}), f32[32,2,64,128]{3,2,1,0:T(8,128)}, u32[]{:S(2)}, u32[]{:S(2)}) async-start(f32[32,2,64,128]{3,2,1,0:T(8,128)} %get-tuple-element.8), calls=%async_computation.2 | async-start | bytes 4194304 | tf_op jit(solution)/shard_map/all_to_all | solution.py:318
  180.9 4.5 %copy-start.5 = (f32[64,64,1]{1,0,2:T(8,128)S(1)}, f32[64,64,1]{1,0,2:T(8,128)}, u32[]{:S(2)}) copy-start(f32[64,64,1]{1,0,2:T(8,128)} %reshape.54) | copy-start | bytes 49156
  183.6 1.9 copy-start.4
